TPU v7x, 32 devices: a whole 2x2x4 slice. The times are simulated.
32 devices in a mesh: grp: 2 (over x), tm: 8 (over z, y), head: 2 (over core).
Axes of the slice: x: 2, y: 2, z: 4, core: 2. Of those that a mesh axis runs over, the one named last changes fastest.
Arguments:
- queries: bfloat16 [2048, 6144], P(('grp', 'tm'), 'head'), parts along dimension 0, may hold values from -130 to 130
- keys: bfloat16 [2048, 1024], P(('grp', 'tm'), 'head'), parts along dimension 0, may hold values from -7 to 7
- values: bfloat16 [2048, 1024], P(('grp', 'tm'), 'head'), parts along dimension 0, may hold values from -6 to 6
- span_mask: int32 [8, 4], P('grp'), parts along dimension 0, may hold values from 0 to 1, as said below
- section: int32 [8], P('grp'), parts along dimension 0, may hold values from 0 to 3
- section_gate: float32 [4, 6144], P(None, 'head'), may hold values from 0.1 to 1.9
Outputs:
- mixed: bfloat16 [2048, 6144], P(('grp', 'tm'), 'head'), parts along dimension 0
- log_total: float32 [48, 2048], P('head', ('grp', 'tm')), parts along dimension 1
There are 2 independent parts, one for each index of `grp`. A program takes and returns all parts, laid end to end along the dimension named above; an argument that names none is the same for every part. Nothing has to cross between parts.
Inputs may be any that keep to these rules, and one draw needn't show every extreme that they name: `span_mask`: the first column and the diagonal are 1 and everything above the diagonal is 0.
All inputs are finite; a program needn't handle non-finite values.
Results may differ from a plain program's by a relative error of at most 0.006.
Values may be sent and summed in bfloat16 or wider, within the bound.
No kernel may reach another device: no remote copies, remote signals or barrier semaphores. Data moves between devices by JAX's collectives and lax.ppermute only.
A program may use at most 64 MiB of HBM per device.

v0:
```python
import math

import jax
import jax.numpy as jnp
from jax import lax
from jax.sharding import PartitionSpec as P

HEAD_SIZE = 128
CH = 256


neg_fill = -1e30


def from_behind(value, axis, steps):
    count = lax.axis_size(axis)
    pairs = [(source, (source + steps) % count) for source in range(count)]
    return lax.ppermute(value, axis, pairs)


def attend_block(carry, grouped, key_block, value_block, allowed, scale):
    run_max, run_total, accum = carry
    kv_heads = run_max.shape[0]
    key_rows = key_block.shape[0]
    keys_three = key_block.reshape(key_rows, kv_heads, HEAD_SIZE)
    values_three = value_block.reshape(key_rows, kv_heads, HEAD_SIZE)
    score = (
        jnp.einsum("qkgd,nkd->kgqn", grouped, keys_three, preferred_element_type=jnp.float32)
        * scale
    )
    score = jnp.where(allowed[None, None], score, neg_fill)
    new_max = jnp.maximum(run_max, jnp.max(score, axis=-1))
    weight = jnp.where(allowed[None, None], jnp.exp(score - new_max[..., None]), 0.0)
    factor = jnp.exp(run_max - new_max)
    new_total = run_total * factor + jnp.sum(weight, axis=-1)
    new_accum = accum * factor[..., None] + jnp.einsum(
        "kgqn,nkd->kgqd",
        weight.astype(jnp.bfloat16),
        values_three,
        preferred_element_type=jnp.float32,
    )
    return (new_max, new_total, new_accum)


def visit_block(carry, grouped, key_block, value_block, allowed, scale):
    return attend_block(carry, grouped, key_block, value_block, allowed, scale)


def on_device(queries, keys, values, span_mask, section, section_gate):
    tok_rows = queries.shape[0]
    kv_local = keys.shape[1] // HEAD_SIZE
    q_local = queries.shape[1] // HEAD_SIZE
    query_group = q_local // kv_local
    scale = 1.0 / math.sqrt(HEAD_SIZE)
    count = lax.axis_size("tm")
    here = lax.axis_index("tm")
    row_ids = jnp.arange(tok_rows, dtype=jnp.int32)
    global_rows = here * tok_rows + row_ids
    query_spans = global_rows // CH
    row_mask = jnp.take(span_mask, query_spans, axis=0)
    grouped = queries.reshape(tok_rows, kv_local, query_group, HEAD_SIZE)
    carry = (
        jnp.full((kv_local, query_group, tok_rows), neg_fill, jnp.float32),
        jnp.zeros((kv_local, query_group, tok_rows), jnp.float32),
        jnp.zeros((kv_local, query_group, tok_rows, HEAD_SIZE), jnp.float32),
    )
    local_spans = (here * tok_rows + row_ids) // CH
    carry = visit_block(
        carry, grouped, keys, values, jnp.take(row_mask, local_spans, axis=1) > 0, scale
    )

    def hop(step, state):
        stacked, inner = state
        stacked = from_behind(stacked, "tm", 1)
        source = (here - step) % count
        key_spans = (source * tok_rows + row_ids) // CH
        inner = visit_block(
            inner, grouped, stacked[0], stacked[1], jnp.take(row_mask, key_spans, axis=1) > 0, scale
        )
        return (stacked, inner)

    stacked, carry = lax.fori_loop(1, count, hop, (jnp.stack([keys, values]), carry))
    run_max, run_total, accum = carry
    attended = jnp.transpose(accum / run_total[..., None], (2, 0, 1, 3)).reshape(
        tok_rows, q_local * HEAD_SIZE
    )
    log_total = (run_max + jnp.log(run_total)).reshape(q_local, tok_rows)
    gate_rows = jnp.take(section_gate, jnp.take(section, query_spans), axis=0)
    mixed = (gate_rows * attended).astype(jnp.bfloat16)
    return (mixed, log_total)


def solution(mesh):
    placed = (
        P(("grp", "tm"), "head"),
        P(("grp", "tm"), "head"),
        P(("grp", "tm"), "head"),
        P("grp", None),
        P("grp"),
        P(None, "head"),
    )
    return jax.shard_map(
        on_device,
        mesh=mesh,
        in_specs=placed,
        out_specs=(P(("grp", "tm"), "head"), P("head", ("grp", "tm"))),
        check_vma=False,
    )
```

profile of v0, /device:TPU:0, one launch (start us, length us, event | category | flops | bytes accessed | tf_op | source)
XLA Modules:
  0.0 97.1 jit_solution(13808914991739466856)
XLA Ops:
  0.7 1.4 %fusion.24 = (s32[1]{0:T(128)}, s32[1]{0:T(128)}, s32[1]{0:T(128)}, s32[1]{0:T(128)}) fusion(s32[4]{0:T(128)} %param.14), kind=kLoop, calls=%fused_computation.71 | loop fusion | bytes 32 | tf_op jit(solution)/shard_map/jit(_take)/gather | solution.py:88
  2.1 2.5 %compare_and_fusion.1 = (pred[128]{0:T(512)(128)(4,1)S(1)}, s32[128]{0:T(128)S(1)}, pred[128]{0:T(512)(128)(4,1)S(1)}) fusion(s32[]{:T(128)S(6)} %mul.77, s32[]{:T(128)} %bitcast.4, s32[]{:T(128)} %bitcast.3, s32[]{:T(128)} %bitcast.2, s32[]{:T(128)} %bitcast.1), kind=kLoop, calls=%fused_computation.55 | loop fusion | flops 6912 | bytes 788 | tf_op jit(solution)/shard_map/jit(_take)/and | solution.py:88
  4.6 1.3 %gather_fusion.2 = s32[128,4]{1,0:T(8,128)S(1)} fusion(s32[4,4]{1,0:T(4,128)} %param.13, s32[1024]{0:T(1024)S(1)} %pad_clamp_fusion.2), kind=kCustom, calls=%fused_computation.3 | custom fusion | bytes 4608 | tf_op jit(solution)/shard_map/jit(_take)/gather | solution.py:60
  6.1 0.6 gather_fusion.3
  6.9 0.4 copy.21
  7.4 0.4 fusion.25
  7.8 0.3 fusion.11
  8.4 0.8 convolution_add_fusion
  9.2 1.6 %copy.27 = bf16[128,4,6,128]{3,0,2,1:T(8,128)(2,1)S(1)} copy(bf16[128,4,6,128]{0,3,2,1:T(8,128)(2,1)} %bitcast.60) | data formatting | bytes 1572864
  11.1 82.1 %while.22 = (s32[]{:T(128)}, bf16[2,128,512]{1,2,0:T(8,128)(2,1)S(1)}, f32[4,6,128]{2,1,0:T(8,128)S(1)}, f32[4,6,128]{2,1,0:T(8,128)S(1)}, f32[4,6,128,128]{3,2,...) while((s32[]{:T(128)}, ...), condition=%wide.region_5.7_spmd.clone, body=%wide.region_2.6_spmd.clone.sunk | while | flops 205697168 | bytes 11474994 | solution.py:82
  11.1 3.0 %collective-permute-start = (bf16[2,128,512]{1,2,0:T(8,128)(2,1)S(1)}, bf16[2,128,512]{1,2,0:T(8,128)(2,1)S(1)}, u32[]{:S(2)}, u32[]{:S(2)}) collective-permute-start(bf16[2,128,512]{1,2,0:T(8,128)(2,1)S(1)} %get-tuple-element.373), channel_id=1, source_target_pairs={{0,2},{2,4},{4,6},{6,8},{8,10},{10,12},{12,14},{14,0},{1,3},{3,5},... | collective-permute-start | bytes 786440 | tf_op jit(solution)/shard_map/while/body/eval_jaxpr/ppermute | solution.py:18
  14.2 0.6 gather_fusion
  14.9 8.6 %collective-permute-done = bf16[2,128,512]{1,2,0:T(8,128)(2,1)S(1)} collective-permute-done((bf16[2,128,512]{1,2,0:T(8,128)(2,1)S(1)}, bf16[2,128,512]{1,2,0:T(8,128)(2,1)S(1)}, u32[]{:S(2)}, u32[]{:S(2)}) %collective-permute-start) | collective-permute-done | bytes 262176 | tf_op jit(solution)/shard_map/while/body/eval_jaxpr/ppermute | solution.py:18
  23.5 0.4 fusion.42
  24.0 0.3 fusion.43
  24.3 1.1 %multiply_add_fusion.5 = f32[4,6,128,128]{3,2,1,0:T(8,128)S(1)} fusion(f32[4,6,128,128]{3,2,1,0:T(8,128)S(1)} %get-tuple-element.376, bf16[128,4,128,1]{0,2,3,1:T(8,128)(2,1)S(1)} %bitcast.57, f32[4,6,128,128]{2,3,1,0:T(8,128)S(1)} %get-tuple-element.355, f32[4,6,128]{2,1,0:T(8,128)S(1)} %get-tuple-element.358, f32[4,6,128]{2,1,0:T(8,128)S(1)} %max.12, ...), kind=kOutput, calls=%fused_computation.6.clone.1 | convolution fusion | flops 102629376 | bytes 4890624 | tf_op jit(solution)/shard_map/while/body/eval_jaxpr/kgqn,nkd->kgqd/dot_general | solution.py:36
  25.6 0.6 gather_fusion
  26.3 9.4 %collective-permute-done = bf16[2,128,512]{1,2,0:T(8,128)(2,1)S(1)} collective-permute-done((bf16[2,128,512]{1,2,0:T(8,128)(2,1)S(1)}, bf16[2,128,512]{1,2,0:T(8,128)(2,1)S(1)}, u32[]{:S(2)}, u32[]{:S(2)}) %collective-permute-start) | collective-permute-done | bytes 262176 | tf_op jit(solution)/shard_map/while/body/eval_jaxpr/ppermute | solution.py:18
  35.7 0.5 fusion.42
  36.2 0.3 fusion.43
  36.5 1.1 %multiply_add_fusion.5 = f32[4,6,128,128]{3,2,1,0:T(8,128)S(1)} fusion(f32[4,6,128,128]{3,2,1,0:T(8,128)S(1)} %get-tuple-element.376, bf16[128,4,128,1]{0,2,3,1:T(8,128)(2,1)S(1)} %bitcast.57, f32[4,6,128,128]{2,3,1,0:T(8,128)S(1)} %get-tuple-element.355, f32[4,6,128]{2,1,0:T(8,128)S(1)} %get-tuple-element.358, f32[4,6,128]{2,1,0:T(8,128)S(1)} %max.12, ...), kind=kOutput, calls=%fused_computation.6.clone.1 | convolution fusion | flops 102629376 | bytes 4890624 | tf_op jit(solution)/shard_map/while/body/eval_jaxpr/kgqn,nkd->kgqd/dot_general | solution.py:36
  37.8 0.6 gather_fusion
  38.5 8.4 %collective-permute-done = bf16[2,128,512]{1,2,0:T(8,128)(2,1)S(1)} collective-permute-done((bf16[2,128,512]{1,2,0:T(8,128)(2,1)S(1)}, bf16[2,128,512]{1,2,0:T(8,128)(2,1)S(1)}, u32[]{:S(2)}, u32[]{:S(2)}) %collective-permute-start) | collective-permute-done | bytes 262176 | tf_op jit(solution)/shard_map/while/body/eval_jaxpr/ppermute | solution.py:18
  47.0 0.4 fusion.42
  47.4 0.3 fusion.43
  47.8 1.1 %multiply_add_fusion.5 = f32[4,6,128,128]{3,2,1,0:T(8,128)S(1)} fusion(f32[4,6,128,128]{3,2,1,0:T(8,128)S(1)} %get-tuple-element.376, bf16[128,4,128,1]{0,2,3,1:T(8,128)(2,1)S(1)} %bitcast.57, f32[4,6,128,128]{2,3,1,0:T(8,128)S(1)} %get-tuple-element.355, f32[4,6,128]{2,1,0:T(8,128)S(1)} %get-tuple-element.358, f32[4,6,128]{2,1,0:T(8,128)S(1)} %max.12, ...), kind=kOutput, calls=%fused_computation.6.clone.1 | convolution fusion | flops 102629376 | bytes 4890624 | tf_op jit(solution)/shard_map/while/body/eval_jaxpr/kgqn,nkd->kgqd/dot_general | solution.py:36
  49.0 0.6 gather_fusion
  49.8 8.2 %collective-permute-done = bf16[2,128,512]{1,2,0:T(8,128)(2,1)S(1)} collective-permute-done((bf16[2,128,512]{1,2,0:T(8,128)(2,1)S(1)}, bf16[2,128,512]{1,2,0:T(8,128)(2,1)S(1)}, u32[]{:S(2)}, u32[]{:S(2)}) %collective-permute-start) | collective-permute-done | bytes 262176 | tf_op jit(solution)/shard_map/while/body/eval_jaxpr/ppermute | solution.py:18
  58.0 0.4 fusion.42
  58.8 1.1 %multiply_add_fusion.5 = f32[4,6,128,128]{3,2,1,0:T(8,128)S(1)} fusion(f32[4,6,128,128]{3,2,1,0:T(8,128)S(1)} %get-tuple-element.376, bf16[128,4,128,1]{0,2,3,1:T(8,128)(2,1)S(1)} %bitcast.57, f32[4,6,128,128]{2,3,1,0:T(8,128)S(1)} %get-tuple-element.355, f32[4,6,128]{2,1,0:T(8,128)S(1)} %get-tuple-element.358, f32[4,6,128]{2,1,0:T(8,128)S(1)} %max.12, ...), kind=kOutput, calls=%fused_computation.6.clone.1 | convolution fusion | flops 102629376 | bytes 4890624 | tf_op jit(solution)/shard_map/while/body/eval_jaxpr/kgqn,nkd->kgqd/dot_general | solution.py:36
  60.1 0.6 gather_fusion
  60.8 8.2 %collective-permute-done = bf16[2,128,512]{1,2,0:T(8,128)(2,1)S(1)} collective-permute-done((bf16[2,128,512]{1,2,0:T(8,128)(2,1)S(1)}, bf16[2,128,512]{1,2,0:T(8,128)(2,1)S(1)}, u32[]{:S(2)}, u32[]{:S(2)}) %collective-permute-start) | collective-permute-done | bytes 262176 | tf_op jit(solution)/shard_map/while/body/eval_jaxpr/ppermute | solution.py:18
  69.1 0.4 fusion.42
  69.9 1.1 %multiply_add_fusion.5 = f32[4,6,128,128]{3,2,1,0:T(8,128)S(1)} fusion(f32[4,6,128,128]{3,2,1,0:T(8,128)S(1)} %get-tuple-element.376, bf16[128,4,128,1]{0,2,3,1:T(8,128)(2,1)S(1)} %bitcast.57, f32[4,6,128,128]{2,3,1,0:T(8,128)S(1)} %get-tuple-element.355, f32[4,6,128]{2,1,0:T(8,128)S(1)} %get-tuple-element.358, f32[4,6,128]{2,1,0:T(8,128)S(1)} %max.12, ...), kind=kOutput, calls=%fused_computation.6.clone.1 | convolution fusion | flops 102629376 | bytes 4890624 | tf_op jit(solution)/shard_map/while/body/eval_jaxpr/kgqn,nkd->kgqd/dot_general | solution.py:36
  71.2 0.6 gather_fusion
  71.9 8.2 %collective-permute-done = bf16[2,128,512]{1,2,0:T(8,128)(2,1)S(1)} collective-permute-done((bf16[2,128,512]{1,2,0:T(8,128)(2,1)S(1)}, bf16[2,128,512]{1,2,0:T(8,128)(2,1)S(1)}, u32[]{:S(2)}, u32[]{:S(2)}) %collective-permute-start) | collective-permute-done | bytes 262176 | tf_op jit(solution)/shard_map/while/body/eval_jaxpr/ppermute | solution.py:18
  80.2 0.4 fusion.42
  80.6 0.3 fusion.43
  81.0 1.1 %multiply_add_fusion.5 = f32[4,6,128,128]{3,2,1,0:T(8,128)S(1)} fusion(f32[4,6,128,128]{3,2,1,0:T(8,128)S(1)} %get-tuple-element.376, bf16[128,4,128,1]{0,2,3,1:T(8,128)(2,1)S(1)} %bitcast.57, f32[4,6,128,128]{2,3,1,0:T(8,128)S(1)} %get-tuple-element.355, f32[4,6,128]{2,1,0:T(8,128)S(1)} %get-tuple-element.358, f32[4,6,128]{2,1,0:T(8,128)S(1)} %max.12, ...), kind=kOutput, calls=%fused_computation.6.clone.1 | convolution fusion | flops 102629376 | bytes 4890624 | tf_op jit(solution)/shard_map/while/body/eval_jaxpr/kgqn,nkd->kgqd/dot_general | solution.py:36
  82.2 0.6 gather_fusion
  83.0 8.2 %collective-permute-done = bf16[2,128,512]{1,2,0:T(8,128)(2,1)S(1)} collective-permute-done((bf16[2,128,512]{1,2,0:T(8,128)(2,1)S(1)}, bf16[2,128,512]{1,2,0:T(8,128)(2,1)S(1)}, u32[]{:S(2)}, u32[]{:S(2)}) %collective-permute-start) | collective-permute-done | bytes 262176 | tf_op jit(solution)/shard_map/while/body/eval_jaxpr/ppermute | solution.py:18
  91.2 0.4 fusion.42
  92.0 1.1 %multiply_add_fusion.5 = f32[4,6,128,128]{3,2,1,0:T(8,128)S(1)} fusion(f32[4,6,128,128]{3,2,1,0:T(8,128)S(1)} %get-tuple-element.376, bf16[128,4,128,1]{0,2,3,1:T(8,128)(2,1)S(1)} %bitcast.57, f32[4,6,128,128]{2,3,1,0:T(8,128)S(1)} %get-tuple-element.355, f32[4,6,128]{2,1,0:T(8,128)S(1)} %get-tuple-element.358, f32[4,6,128]{2,1,0:T(8,128)S(1)} %max.12, ...), kind=kOutput, calls=%fused_computation.6.clone.1 | convolution fusion | flops 102629376 | bytes 4890624 | tf_op jit(solution)/shard_map/while/body/eval_jaxpr/kgqn,nkd->kgqd/dot_general | solution.py:36
  93.2 0.6 reshape.138
  93.8 0.5 copy.28
  94.4 0.5 copy.29
  95.0 1.0 %gather_fusion.1 = f32[128,3072]{1,0:T(8,128)S(1)} fusion(f32[4,3072]{1,0:T(4,128)S(1)} %copy-done, s32[1024]{0:T(1024)S(1)} %pad_clamp_fusion.3), kind=kCustom, calls=%fused_computation.2 | custom fusion | bytes 3146240 | tf_op jit(solution)/shard_map/jit(_take)/gather | solution.py:88
  95.9 1.1 %multiply_convert_fusion = bf16[128,3072]{1,0:T(8,128)(2,1)} fusion(f32[128,3072]{1,0:T(8,128)S(1)} %copy.29, f32[128,3072]{1,0:T(8,128)S(1)} %gather_fusion.1, pred[128]{0:T(512)(128)(4,1)S(1)} %get-tuple-element.283), kind=kLoop, calls=%fused_computation.27 | loop fusion | flops 1179648 | bytes 3932288 | tf_op jit(solution)/shard_map/convert_element_type | solution.py:89
  (102 shorter events, 3.7 us)
Async XLA Ops:
  0.6 94.3 %copy-start = (f32[4,3072]{1,0:T(4,128)S(1)}, f32[4,3072]{1,0:T(4,128)}, u32[]{:S(2)}) copy-start(f32[4,3072]{1,0:T(4,128)} %param.15) | copy-start | bytes 147460
  0.6 6.2 %copy-start.2 = (bf16[128,3072]{1,0:T(8,128)(2,1)S(1)}, bf16[128,3072]{1,0:T(8,128)(2,1)}, u32[]{:S(2)}) copy-start(bf16[128,3072]{1,0:T(8,128)(2,1)} %param.10) | copy-start | bytes 2359300
  0.7 6.6 %copy-start.3 = (bf16[128,512]{1,0:T(8,128)(2,1)S(1)}, bf16[128,512]{1,0:T(8,128)(2,1)}, u32[]{:S(2)}) copy-start(bf16[128,512]{1,0:T(8,128)(2,1)} %param.11) | copy-start | bytes 393220
  7.3 0.9 copy-start.1
  7.3 1.1 %copy-start.4 = (bf16[128,512]{1,0:T(8,128)(2,1)S(1)}, bf16[128,512]{1,0:T(8,128)(2,1)}, u32[]{:S(2)}) copy-start(bf16[128,512]{1,0:T(8,128)(2,1)} %param.12) | copy-start | bytes 393220
  9.2 1.7 %copy-start.5 = (bf16[128,512]{1,0:T(8,128)(2,1)S(1)}, bf16[128,512]{1,0:T(8,128)(2,1)}, u32[]{:S(2)}) copy-start(bf16[128,512]{1,0:T(8,128)(2,1)} %param.12) | copy-start | bytes 393220
  11.1 12.4 %collective-permute-start = (bf16[2,128,512]{1,2,0:T(8,128)(2,1)S(1)}, bf16[2,128,512]{1,2,0:T(8,128)(2,1)S(1)}, u32[]{:S(2)}, u32[]{:S(2)}) collective-permute-start(bf16[2,128,512]{1,2,0:T(8,128)(2,1)S(1)} %get-tuple-element.373), channel_id=1, source_target_pairs={{0,2},{2,4},{4,6},{6,8},{8,10},{10,12},{12,14},{14,0},{1,3},{3,5},... | collective-permute-start | bytes 786440 | tf_op jit(solution)/shard_map/while/body/eval_jaxpr/ppermute | solution.py:18
  25.4 10.2 %collective-permute-start = (bf16[2,128,512]{1,2,0:T(8,128)(2,1)S(1)}, bf16[2,128,512]{1,2,0:T(8,128)(2,1)S(1)}, u32[]{:S(2)}, u32[]{:S(2)}) collective-permute-start(bf16[2,128,512]{1,2,0:T(8,128)(2,1)S(1)} %get-tuple-element.373), channel_id=1, source_target_pairs={{0,2},{2,4},{4,6},{6,8},{8,10},{10,12},{12,14},{14,0},{1,3},{3,5},... | collective-permute-start | bytes 786440 | tf_op jit(solution)/shard_map/while/body/eval_jaxpr/ppermute | solution.py:18
  37.6 9.3 %collective-permute-start = (bf16[2,128,512]{1,2,0:T(8,128)(2,1)S(1)}, bf16[2,128,512]{1,2,0:T(8,128)(2,1)S(1)}, u32[]{:S(2)}, u32[]{:S(2)}) collective-permute-start(bf16[2,128,512]{1,2,0:T(8,128)(2,1)S(1)} %get-tuple-element.373), channel_id=1, source_target_pairs={{0,2},{2,4},{4,6},{6,8},{8,10},{10,12},{12,14},{14,0},{1,3},{3,5},... | collective-permute-start | bytes 786440 | tf_op jit(solution)/shard_map/while/body/eval_jaxpr/ppermute | solution.py:18
  48.9 9.1 %collective-permute-start = (bf16[2,128,512]{1,2,0:T(8,128)(2,1)S(1)}, bf16[2,128,512]{1,2,0:T(8,128)(2,1)S(1)}, u32[]{:S(2)}, u32[]{:S(2)}) collective-permute-start(bf16[2,128,512]{1,2,0:T(8,128)(2,1)S(1)} %get-tuple-element.373), channel_id=1, source_target_pairs={{0,2},{2,4},{4,6},{6,8},{8,10},{10,12},{12,14},{14,0},{1,3},{3,5},... | collective-permute-start | bytes 786440 | tf_op jit(solution)/shard_map/while/body/eval_jaxpr/ppermute | solution.py:18
  60.0 9.1 %collective-permute-start = (bf16[2,128,512]{1,2,0:T(8,128)(2,1)S(1)}, bf16[2,128,512]{1,2,0:T(8,128)(2,1)S(1)}, u32[]{:S(2)}, u32[]{:S(2)}) collective-permute-start(bf16[2,128,512]{1,2,0:T(8,128)(2,1)S(1)} %get-tuple-element.373), channel_id=1, source_target_pairs={{0,2},{2,4},{4,6},{6,8},{8,10},{10,12},{12,14},{14,0},{1,3},{3,5},... | collective-permute-start | bytes 786440 | tf_op jit(solution)/shard_map/while/body/eval_jaxpr/ppermute | solution.py:18
  71.0 9.1 %collective-permute-start = (bf16[2,128,512]{1,2,0:T(8,128)(2,1)S(1)}, bf16[2,128,512]{1,2,0:T(8,128)(2,1)S(1)}, u32[]{:S(2)}, u32[]{:S(2)}) collective-permute-start(bf16[2,128,512]{1,2,0:T(8,128)(2,1)S(1)} %get-tuple-element.373), channel_id=1, source_target_pairs={{0,2},{2,4},{4,6},{6,8},{8,10},{10,12},{12,14},{14,0},{1,3},{3,5},... | collective-permute-start | bytes 786440 | tf_op jit(solution)/shard_map/while/body/eval_jaxpr/ppermute | solution.py:18
  82.1 9.1 %collective-permute-start = (bf16[2,128,512]{1,2,0:T(8,128)(2,1)S(1)}, bf16[2,128,512]{1,2,0:T(8,128)(2,1)S(1)}, u32[]{:S(2)}, u32[]{:S(2)}) collective-permute-start(bf16[2,128,512]{1,2,0:T(8,128)(2,1)S(1)} %get-tuple-element.373), channel_id=1, source_target_pairs={{0,2},{2,4},{4,6},{6,8},{8,10},{10,12},{12,14},{14,0},{1,3},{3,5},... | collective-permute-start | bytes 786440 | tf_op jit(solution)/shard_map/while/body/eval_jaxpr/ppermute | solution.py:18
where the time goes:
time: 97.3 us; the launch traced here: 97.1 us
  waiting for transfers between devices  59.3 us (61%)
  local copies, waits for them, and re-layouts  13.4 us (14%)
  matrix products  11.9 us (12%)
  other arithmetic  7.4 us (8%)
  starting transfers between devices  3.37 us (3%)
    ppermute x7, waiting for transfers between devices, from_behind(): return lax.ppermute(value, axis, pairs)  59.3 us
    dot_general x8, matrix products, attend_block(): jnp.einsum('kgqn,nkd->kgqd', weight.astype(jnp.bfloat16), values_three, p...  8.37 us
    gather x7, local copies, waits for them, and re-layouts, hop(): jnp.take(row_mask, key_spans, axis=1) > 0  4.51 us
    dot_general x8, matrix products, attend_block(): jnp.einsum('qkgd,nkd->kgqn', grouped, keys_three, preferred_element_type=...  3.51 us
    ppermute x7, starting transfers between devices, from_behind(): return lax.ppermute(value, axis, pairs)  3.37 us
    unnamed x16, local copies, waits for them, and re-layouts  2.59 us
    and x1, other arithmetic, on_device(): gate_rows = jnp.take(section_gate, jnp.take(section, query_spans), axis=0)  2.49 us
    gather x2, local copies, waits for them, and re-layouts, on_device(): gate_rows = jnp.take(section_gate, jnp.take(section, query_spans), axis=0)  2.38 us
  transfers between devices with their start and end apart: 7, of which 7 were waited for; matrix products, arithmetic and copies ran while one was open for 6% of the time, Pallas kernels for 0%

commit v1 on v0

v1 whole, which is shorter than its diff:
```python
import functools
import math

import jax
import jax.numpy as jnp
from jax import lax
from jax.experimental import pallas as pl
from jax.experimental.pallas import tpu as pltpu
from jax.sharding import PartitionSpec as P

HEAD_SIZE = 128
CH = 256
LOG2E = math.log2(math.e)
LN2 = math.log(2.0)


def attend_kernel(items, per_span, first, last, refs_in, refs_out):
    refs = list(refs_in)
    mask_ref, section_ref, q_ref = refs[:3]
    refs = refs[3:]
    if last:
        gate_ref = refs.pop(0)
    if not first:
        acc_in, stat_in = refs.pop(0), refs.pop(0)
    key_refs, value_refs = refs[: len(items)], refs[len(items) :]
    if last:
        mixed_ref, log_ref, acc, stat = refs_out
    else:
        acc, stat = refs_out
    rows = q_ref.shape[0]
    kv_heads = acc.shape[0]
    group = q_ref.shape[1] // HEAD_SIZE // kv_heads
    span = lax.axis_index("tm") // per_span
    scale = LOG2E / math.sqrt(HEAD_SIZE)

    if first:
        for h in range(kv_heads):
            stat[h, 0:1, :] = jnp.full((1, group * rows), -1e30, jnp.float32)
            stat[h, 1:2, :] = jnp.zeros((1, group * rows), jnp.float32)
            acc[h] = jnp.zeros(acc.shape[1:], jnp.float32)
    else:
        for h in range(kv_heads):
            stat[h, 0:2, :] = stat_in[h, 0:2, :]
            acc[h] = acc_in[h]

    def visit(k_ref, v_ref):
        for h in range(kv_heads):
            queries = jnp.concatenate(
                [q_ref[:, (h * group + g) * HEAD_SIZE : (h * group + g + 1) * HEAD_SIZE] for g in range(group)], axis=0
            )
            k = k_ref[:, h * HEAD_SIZE : (h + 1) * HEAD_SIZE]
            v = v_ref[:, h * HEAD_SIZE : (h + 1) * HEAD_SIZE]
            score = scale * lax.dot_general(k, queries, (((1,), (1,)), ((), ())), preferred_element_type=jnp.float32)
            old = stat[h, 0:1, :]
            top = jnp.maximum(old, jnp.max(score, axis=0, keepdims=True))
            weight = jnp.exp2(score - top)
            factor = jnp.exp2(old - top)
            stat[h, 0:1, :] = top
            stat[h, 1:2, :] = stat[h, 1:2, :] * factor + jnp.sum(weight, axis=0, keepdims=True)
            part = lax.dot_general(
                v, weight.astype(jnp.bfloat16), (((0,), (0,)), ((), ())), preferred_element_type=jnp.float32
            )
            acc[h] = acc[h] * factor + part

    for distance, k_ref, v_ref in zip(items, key_refs, value_refs):
        if distance == 0:
            visit(k_ref, v_ref)
        else:
            behind = jnp.maximum(span - distance, 0)
            seen = jnp.logical_and(span >= distance, mask_ref[span, behind] > 0)
            pl.when(seen)(functools.partial(visit, k_ref, v_ref))

    if last:
        gate_row = gate_ref[pl.ds(section_ref[span], 1), :]
        for h in range(kv_heads):
            total = stat[h, 1:2, :]
            log_total = stat[h, 0:1, :] * LN2 + jnp.log(total)
            attended = acc[h] / total
            for g in range(group):
                head = h * group + g
                columns = slice(head * HEAD_SIZE, (head + 1) * HEAD_SIZE)
                block = attended[:, g * rows : (g + 1) * rows].T
                mixed_ref[:, columns] = (gate_row[:, columns] * block).astype(jnp.bfloat16)
                log_ref[head : head + 1, :] = log_total[:, g * rows : (g + 1) * rows]


def attend(name, items, per_span, state, last, mask, section, queries, gate, kv_heads):
    rows, width = queries.shape
    heads = width // HEAD_SIZE
    group = heads // kv_heads
    first = state is None
    operands = [mask, section, queries]
    specs = [pl.BlockSpec(memory_space=pltpu.SMEM)] * 2 + [pl.BlockSpec(memory_space=pltpu.VMEM)]
    if last:
        operands.append(gate)
    if not first:
        operands += list(state)
    operands += [k for _, k, _ in items] + [v for _, _, v in items]
    specs += [pl.BlockSpec(memory_space=pltpu.VMEM)] * (len(operands) - len(specs))
    acc_shape = (kv_heads, HEAD_SIZE, group * rows)
    stat_shape = (kv_heads, 8, group * rows)
    scratch = []
    if last:
        out_shape = (
            jax.ShapeDtypeStruct((rows, width), jnp.bfloat16),
            jax.ShapeDtypeStruct((heads, rows), jnp.float32),
        )
        scratch = [pltpu.VMEM(acc_shape, jnp.float32), pltpu.VMEM(stat_shape, jnp.float32)]
    else:
        out_shape = (
            jax.ShapeDtypeStruct(acc_shape, jnp.float32),
            jax.ShapeDtypeStruct(stat_shape, jnp.float32),
        )
    count = len(operands)

    def kernel(*refs):
        attend_kernel([d for d, _, _ in items], per_span, first, last, refs[:count], refs[count:])

    keys_seen = len(items) * rows
    return pl.pallas_call(
        kernel,
        out_shape=out_shape,
        in_specs=specs,
        out_specs=(pl.BlockSpec(memory_space=pltpu.VMEM),) * 2,
        scratch_shapes=scratch,
        compiler_params=pltpu.CompilerParams(vmem_limit_bytes=24 * 1024 * 1024),
        cost_estimate=pl.CostEstimate(
            flops=8 * keys_seen * rows * width,
            bytes_accessed=rows * width * 8,
            transcendentals=keys_seen * rows * heads,
        ),
        name=name,
    )(*operands)


def on_device(queries, keys, values, span_mask, section, section_gate):
    rows = queries.shape[0]
    kv_heads = keys.shape[1] // HEAD_SIZE
    count = lax.axis_size("tm")
    per_span = CH // rows
    spans = count // per_span

    def onward(value, distance):
        pairs = [(i, i + per_span) for i in range((distance - 1) * per_span, count - per_span)]
        return lax.ppermute(value, "tm", pairs)

    def around(value, distance, turn):
        pairs = [
            (s * per_span + i, s * per_span + (i + turn) % per_span)
            for s in range(distance, spans)
            for i in range(per_span)
        ]
        return lax.ppermute(value, "tm", pairs)

    blocks = []
    held = (keys, values)
    for distance in range(spans):
        if distance:
            held = tuple(onward(x, distance) for x in held)
        blocks.append((distance, 0, held))
        for turn in range(1, per_span):
            blocks.append((distance, turn, tuple(around(x, distance, turn) for x in held)))
    blocks.sort(key=lambda b: (b[0] + (b[1] > 0), -b[1]))
    blocks = [(d, k, v) for d, _, (k, v) in blocks]
    groups = [blocks[i : i + 3] for i in range(0, len(blocks) - 1, 3)]
    groups[-1] = [b for b in groups[-1] if b is not blocks[-1]]
    groups.append([blocks[-1]])
    groups = [g for g in groups if g]
    state = None
    for at, group in enumerate(groups):
        state = attend(
            "attend_%d" % at, group, per_span, state, at == len(groups) - 1,
            span_mask, section, queries, section_gate, kv_heads,
        )
    return state


def solution(mesh):
    placed = (
        P(("grp", "tm"), "head"),
        P(("grp", "tm"), "head"),
        P(("grp", "tm"), "head"),
        P("grp", None),
        P("grp"),
        P(None, "head"),
    )
    return jax.shard_map(
        on_device,
        mesh=mesh,
        in_specs=placed,
        out_specs=(P(("grp", "tm"), "head"), P("head", ("grp", "tm"))),
        check_vma=False,
    )
```

time: 97.3 us -> 53.9 us (0.55)
  the two profiles are of different devices: /device:TPU:0 before, /device:TPU:24 now
where the time goes in v1:
time: 53.9 us; the launch traced here: 53.4 us
  starting transfers between devices  28.4 us (53%)
  Pallas kernels  15.2 us (28%)
  waiting for transfers between devices  4.71 us (9%)
  local copies, waits for them, and re-layouts  4.28 us (8%)
  between operations  0.87 us (2%)
    ppermute x8, starting transfers between devices, around(): return lax.ppermute(value, 'tm', pairs)  20.7 us
    pallas_call x4, Pallas kernels, attend(): pl.pallas_call(kernel, out_shape=out_shape, in_specs=specs, out_specs=(pl...  15.2 us
    ppermute x6, starting transfers between devices, onward(): return lax.ppermute(value, 'tm', pairs)  7.73 us
    ppermute x6, waiting for transfers between devices, onward(): return lax.ppermute(value, 'tm', pairs)  4.69 us
    unnamed x12, local copies, waits for them, and re-layouts  4.28 us
  transfers between devices with their start and end apart: 14, of which 2 were waited for; matrix products, arithmetic and copies ran while one was open for 0% of the time, Pallas kernels for 22%

profile of v1, /device:TPU:24, one launch (start us, length us, event | category | flops | bytes accessed | tf_op | source)
XLA Modules:
  0.0 53.4 jit_solution(1683670034945961953)
XLA Ops:
  0.6 1.3 %collective-permute-start.1 = (bf16[128,512]{1,0:T(8,128)(2,1)}, bf16[128,512]{1,0:T(8,128)(2,1)S(1)}, u32[]{:S(2)}, u32[]{:S(2)}) collective-permute-start(bf16[128,512]{1,0:T(8,128)(2,1)} %refs_3_.2), channel_id=1, source_target_pairs={{0,4},{2,6},{4,8},{6,10},{8,12},{10,14},{1,5},{3,7},{5,9},{7,11},{... | collective-permute-start | bytes 393224 | tf_op jit(solution)/shard_map/ppermute | solution.py:145
  1.9 1.3 %collective-permute-start.3 = (bf16[128,512]{1,0:T(8,128)(2,1)}, bf16[128,512]{1,0:T(8,128)(2,1)S(1)}, u32[]{:S(2)}, u32[]{:S(2)}) collective-permute-start(bf16[128,512]{1,0:T(8,128)(2,1)} %refs_6_.1), channel_id=1, source_target_pairs={{0,4},{2,6},{4,8},{6,10},{8,12},{10,14},{1,5},{3,7},{5,9},{7,11},{... | collective-permute-start | bytes 393224 | tf_op jit(solution)/shard_map/ppermute | solution.py:145
  3.2 1.6 %collective-permute-start = (bf16[128,512]{1,0:T(8,128)(2,1)}, bf16[128,512]{1,0:T(8,128)(2,1)S(1)}, u32[]{:S(2)}, u32[]{:S(2)}) collective-permute-start(bf16[128,512]{1,0:T(8,128)(2,1)} %refs_3_.2), channel_id=1, source_target_pairs={{0,2},{2,0},{4,6},{6,4},{8,10},{10,8},{12,14},{14,12},{1,3},{3,1},... | collective-permute-start | bytes 393224 | tf_op jit(solution)/shard_map/ppermute | solution.py:153
  4.8 4.1 %collective-permute-done.1.refs_5_ = bf16[128,512]{1,0:T(8,128)(2,1)S(1)} collective-permute-done((bf16[128,512]{1,0:T(8,128)(2,1)}, bf16[128,512]{1,0:T(8,128)(2,1)S(1)}, u32[]{:S(2)}, u32[]{:S(2)}) %collective-permute-start.1) | collective-permute-done | bytes 131104 | tf_op jit(solution)/shard_map/ppermute | solution.py:145
  8.9 1.3 %collective-permute-start.5 = (bf16[128,512]{1,0:T(8,128)(2,1)S(1)}, bf16[128,512]{1,0:T(8,128)(2,1)S(1)}, u32[]{:S(2)}, u32[]{:S(2)}) collective-permute-start(bf16[128,512]{1,0:T(8,128)(2,1)S(1)} %collective-permute-done.1.refs_5_), channel_id=1, source_target_pairs={{4,8},{6,10},{8,12},{10,14},{5,9},{7,11},{9,13},{11,15},{20,24},{2... | collective-permute-start | bytes 393224 | tf_op jit(solution)/shard_map/ppermute | solution.py:145
  10.2 0.6 %collective-permute-done.3.refs_8_ = bf16[128,512]{1,0:T(8,128)(2,1)S(1)} collective-permute-done((bf16[128,512]{1,0:T(8,128)(2,1)}, bf16[128,512]{1,0:T(8,128)(2,1)S(1)}, u32[]{:S(2)}, u32[]{:S(2)}) %collective-permute-start.3) | collective-permute-done | bytes 131104 | tf_op jit(solution)/shard_map/ppermute | solution.py:145
  10.8 1.3 %collective-permute-start.8 = (bf16[128,512]{1,0:T(8,128)(2,1)S(1)}, bf16[128,512]{1,0:T(8,128)(2,1)S(1)}, u32[]{:S(2)}, u32[]{:S(2)}) collective-permute-start(bf16[128,512]{1,0:T(8,128)(2,1)S(1)} %collective-permute-done.3.refs_8_), channel_id=1, source_target_pairs={{4,8},{6,10},{8,12},{10,14},{5,9},{7,11},{9,13},{11,15},{20,24},{2... | collective-permute-start | bytes 393224 | tf_op jit(solution)/shard_map/ppermute | solution.py:145
  12.1 1.6 %collective-permute-start.2 = (bf16[128,512]{1,0:T(8,128)(2,1)}, bf16[128,512]{1,0:T(8,128)(2,1)S(1)}, u32[]{:S(2)}, u32[]{:S(2)}) collective-permute-start(bf16[128,512]{1,0:T(8,128)(2,1)} %refs_6_.1), channel_id=1, source_target_pairs={{0,2},{2,0},{4,6},{6,4},{8,10},{10,8},{12,14},{14,12},{1,3},{3,1},... | collective-permute-start | bytes 393224 | tf_op jit(solution)/shard_map/ppermute | solution.py:153
  13.7 2.4 %collective-permute-start.4 = (bf16[128,512]{1,0:T(8,128)(2,1)S(1)}, bf16[128,512]{1,0:T(8,128)(2,1)S(1)}, u32[]{:S(2)}, u32[]{:S(2)}) collective-permute-start(bf16[128,512]{1,0:T(8,128)(2,1)S(1)} %collective-permute-done.1.refs_5_), channel_id=1, source_target_pairs={{4,6},{6,4},{8,10},{10,8},{12,14},{14,12},{5,7},{7,5},{9,11},{11,9... | collective-permute-start | bytes 393224 | tf_op jit(solution)/shard_map/ppermute | solution.py:153
  16.1 0.0 collective-permute-done.refs_4_
  16.1 3.4 %collective-permute-start.7 = (bf16[128,512]{1,0:T(8,128)(2,1)S(1)}, bf16[128,512]{1,0:T(8,128)(2,1)S(1)}, u32[]{:S(2)}, u32[]{:S(2)}) collective-permute-start(bf16[128,512]{1,0:T(8,128)(2,1)S(1)} %collective-permute-done.3.refs_8_), channel_id=1, source_target_pairs={{4,6},{6,4},{8,10},{10,8},{12,14},{14,12},{5,7},{7,5},{9,11},{11,9... | collective-permute-start | bytes 393224 | tf_op jit(solution)/shard_map/ppermute | solution.py:153
  19.5 0.0 collective-permute-done.5.refs_6_
  19.5 1.3 %collective-permute-start.10 = (bf16[128,512]{1,0:T(8,128)(2,1)S(1)}, bf16[128,512]{1,0:T(8,128)(2,1)S(1)}, u32[]{:S(2)}, u32[]{:S(2)}) collective-permute-start(bf16[128,512]{1,0:T(8,128)(2,1)S(1)} %collective-permute-done.5.refs_6_), channel_id=1, source_target_pairs={{8,12},{10,14},{9,13},{11,15},{24,28},{26,30},{25,29},{27,31}} | collective-permute-start | bytes 393224 | tf_op jit(solution)/shard_map/ppermute | solution.py:145
  20.8 0.0 collective-permute-done.8.refs_9_
  20.8 1.3 %collective-permute-start.11 = (bf16[128,512]{1,0:T(8,128)(2,1)S(1)}, bf16[128,512]{1,0:T(8,128)(2,1)S(1)}, u32[]{:S(2)}, u32[]{:S(2)}) collective-permute-start(bf16[128,512]{1,0:T(8,128)(2,1)S(1)} %collective-permute-done.8.refs_9_), channel_id=1, source_target_pairs={{8,12},{10,14},{9,13},{11,15},{24,28},{26,30},{25,29},{27,31}} | collective-permute-start | bytes 393224 | tf_op jit(solution)/shard_map/ppermute | solution.py:145
  22.1 0.0 collective-permute-done.2.refs_7_
  22.1 2.4 %collective-permute-start.6 = (bf16[128,512]{1,0:T(8,128)(2,1)S(1)}, bf16[128,512]{1,0:T(8,128)(2,1)S(1)}, u32[]{:S(2)}, u32[]{:S(2)}) collective-permute-start(bf16[128,512]{1,0:T(8,128)(2,1)S(1)} %collective-permute-done.5.refs_6_), channel_id=1, source_target_pairs={{8,10},{10,8},{12,14},{14,12},{9,11},{11,9},{13,15},{15,13},{24,26... | collective-permute-start | bytes 393224 | tf_op jit(solution)/shard_map/ppermute | solution.py:153
  24.6 0.0 collective-permute-done.4.refs_5_
  24.6 3.4 %collective-permute-start.9 = (bf16[128,512]{1,0:T(8,128)(2,1)S(1)}, bf16[128,512]{1,0:T(8,128)(2,1)S(1)}, u32[]{:S(2)}, u32[]{:S(2)}) collective-permute-start(bf16[128,512]{1,0:T(8,128)(2,1)S(1)} %collective-permute-done.8.refs_9_), channel_id=1, source_target_pairs={{8,10},{10,8},{12,14},{14,12},{9,11},{11,9},{13,15},{15,13},{24,26... | collective-permute-start | bytes 393224 | tf_op jit(solution)/shard_map/ppermute | solution.py:153
  28.0 0.0 copy-start
  28.0 1.1 %copy-done = bf16[128,3072]{1,0:T(8,128)(2,1)S(1)} copy-done((bf16[128,3072]{1,0:T(8,128)(2,1)S(1)}, bf16[128,3072]{1,0:T(8,128)(2,1)}, u32[]{:S(2)}) %copy-start) | copy-done | bytes 786456
  29.1 0.0 copy-start.2
  29.1 0.7 %copy-done.2 = s32[4,4]{1,0:T(4,128)S(1)} copy-done((s32[4,4]{1,0:T(4,128)S(1)}, s32[4,4]{1,0:T(4,128)}, u32[]{:S(2)}) %copy-start.2) | copy-done | bytes 88
  29.8 0.0 copy-start.3
  29.8 0.7 %copy-done.3 = s32[4]{0:T(128)S(1)} copy-done((s32[4]{0:T(128)S(1)}, s32[4]{0:T(128)}, u32[]{:S(2)}) %copy-start.3) | copy-done | bytes 40
  30.5 0.0 copy-start.4
  30.5 0.9 %copy-done.4 = bf16[128,512]{1,0:T(8,128)(2,1)S(1)} copy-done((bf16[128,512]{1,0:T(8,128)(2,1)S(1)}, bf16[128,512]{1,0:T(8,128)(2,1)}, u32[]{:S(2)}) %copy-start.4) | copy-done | bytes 131096
  31.4 0.0 copy-start.5
  31.4 0.9 %copy-done.5 = bf16[128,512]{1,0:T(8,128)(2,1)S(1)} copy-done((bf16[128,512]{1,0:T(8,128)(2,1)S(1)}, bf16[128,512]{1,0:T(8,128)(2,1)}, u32[]{:S(2)}) %copy-start.5) | copy-done | bytes 131096
  32.3 4.6 %attend_0.1 = (f32[4,128,768]{2,1,0:T(8,128)S(1)}, f32[4,8,768]{2,1,0:T(8,128)S(1)}) custom-call(s32[4,4]{1,0:T(4,128)S(1)} %copy-done.2, s32[4]{0:T(128)S(1)} %copy-done.3, bf16[128,3072]{1,0:T(8,128)(2,1)S(1)} %copy-done, bf16[128,512]{1,0:T(8,128)(2,1)S(1)} %copy-done.4, bf16[128,512]{1,0:T(8,128)(2,1)S(1)} %collective-permute-done.refs_4_, ...), custom_call_target="tpu_custom_call" | custom-call | flops 1207959552 | bytes 3145728 | tf_op jit(solution)/shard_map/attend_0/pallas_call | solution.py:120
  36.9 0.0 collective-permute-done.10.refs_5_
  37.0 2.4 %collective-permute-start.12 = (bf16[128,512]{1,0:T(8,128)(2,1)S(1)}, bf16[128,512]{1,0:T(8,128)(2,1)S(1)}, u32[]{:S(2)}, u32[]{:S(2)}) collective-permute-start(bf16[128,512]{1,0:T(8,128)(2,1)S(1)} %collective-permute-done.10.refs_5_), channel_id=1, source_target_pairs={{12,14},{14,12},{13,15},{15,13},{28,30},{30,28},{29,31},{31,29}} | collective-permute-start | bytes 393224 | tf_op jit(solution)/shard_map/ppermute | solution.py:153
  39.4 0.0 collective-permute-done.11.refs_6_
  39.4 3.4 %collective-permute-start.13 = (bf16[128,512]{1,0:T(8,128)(2,1)S(1)}, bf16[128,512]{1,0:T(8,128)(2,1)S(1)}, u32[]{:S(2)}, u32[]{:S(2)}) collective-permute-start(bf16[128,512]{1,0:T(8,128)(2,1)S(1)} %collective-permute-done.11.refs_6_), channel_id=1, source_target_pairs={{12,14},{14,12},{13,15},{15,13},{28,30},{30,28},{29,31},{31,29}} | collective-permute-start | bytes 393224 | tf_op jit(solution)/shard_map/ppermute | solution.py:153
  42.8 0.0 collective-permute-done.7.refs_8_
  42.8 0.0 collective-permute-done.6.refs_7_
  42.8 0.0 collective-permute-done.9.refs_10_
  42.9 4.9 %attend_1.1 = (f32[4,128,768]{2,1,0:T(8,128)S(1)}, f32[4,8,768]{2,1,0:T(8,128)S(1)}) custom-call(s32[4,4]{1,0:T(4,128)S(1)} %copy-done.2, s32[4]{0:T(128)S(1)} %copy-done.3, bf16[128,3072]{1,0:T(8,128)(2,1)S(1)} %copy-done, f32[4,128,768]{2,1,0:T(8,128)S(1)} %get-tuple-element.8.refs_3_, f32[4,8,768]{2,1,0:T(8,128)S(1)} %get-tuple-element.9.refs_4_, ...), custom_call_target="tpu_custom_call" | custom-call | flops 1207959552 | bytes 3145728 | tf_op jit(solution)/shard_map/attend_1/pallas_call | solution.py:120
  47.8 0.0 copy-start.1
  47.8 2.1 %attend_2.1 = (f32[4,128,768]{2,1,0:T(8,128)S(1)}, f32[4,8,768]{2,1,0:T(8,128)S(1)}) custom-call(s32[4,4]{1,0:T(4,128)S(1)} %copy-done.2, s32[4]{0:T(128)S(1)} %copy-done.3, bf16[128,3072]{1,0:T(8,128)(2,1)S(1)} %copy-done, f32[4,128,768]{2,1,0:T(8,128)S(1)} %get-tuple-element.10.refs_3_, f32[4,8,768]{2,1,0:T(8,128)S(1)} %get-tuple-element.11.refs_4_, ...), custom_call_target="tpu_custom_call" | custom-call | flops 402653184 | bytes 3145728 | tf_op jit(solution)/shard_map/attend_2/pallas_call | solution.py:120
  49.9 0.0 collective-permute-done.12.refs_6_
  49.9 0.0 collective-permute-done.13.refs_7_
  49.9 0.0 copy-done.1
  50.0 3.5 %attend_3.1 = (bf16[128,3072]{1,0:T(8,128)(2,1)}, f32[24,128]{1,0:T(8,128)}) custom-call(s32[4,4]{1,0:T(4,128)S(1)} %copy-done.2, s32[4]{0:T(128)S(1)} %copy-done.3, bf16[128,3072]{1,0:T(8,128)(2,1)S(1)} %copy-done, f32[4,3072]{1,0:T(4,128)S(1)} %copy-done.1, f32[4,128,768]{2,1,0:T(8,128)S(1)} %get-tuple-element.12.refs_4_, ...), custom_call_target="tpu_custom_call" | custom-call | flops 402653184 | bytes 3145728 | tf_op jit(solution)/shard_map/attend_3/pallas_call | solution.py:120
Async XLA Ops:
  0.6 8.3 %collective-permute-start.1 = (bf16[128,512]{1,0:T(8,128)(2,1)}, bf16[128,512]{1,0:T(8,128)(2,1)S(1)}, u32[]{:S(2)}, u32[]{:S(2)}) collective-permute-start(bf16[128,512]{1,0:T(8,128)(2,1)} %refs_3_.2), channel_id=1, source_target_pairs={{0,4},{2,6},{4,8},{6,10},{8,12},{10,14},{1,5},{3,7},{5,9},{7,11},{... | collective-permute-start | bytes 393224 | tf_op jit(solution)/shard_map/ppermute | solution.py:145
  1.9 8.8 %collective-permute-start.3 = (bf16[128,512]{1,0:T(8,128)(2,1)}, bf16[128,512]{1,0:T(8,128)(2,1)S(1)}, u32[]{:S(2)}, u32[]{:S(2)}) collective-permute-start(bf16[128,512]{1,0:T(8,128)(2,1)} %refs_6_.1), channel_id=1, source_target_pairs={{0,4},{2,6},{4,8},{6,10},{8,12},{10,14},{1,5},{3,7},{5,9},{7,11},{... | collective-permute-start | bytes 393224 | tf_op jit(solution)/shard_map/ppermute | solution.py:145
  3.2 12.8 %collective-permute-start = (bf16[128,512]{1,0:T(8,128)(2,1)}, bf16[128,512]{1,0:T(8,128)(2,1)S(1)}, u32[]{:S(2)}, u32[]{:S(2)}) collective-permute-start(bf16[128,512]{1,0:T(8,128)(2,1)} %refs_3_.2), channel_id=1, source_target_pairs={{0,2},{2,0},{4,6},{6,4},{8,10},{10,8},{12,14},{14,12},{1,3},{3,1},... | collective-permute-start | bytes 393224 | tf_op jit(solution)/shard_map/ppermute | solution.py:153
  8.9 10.6 %collective-permute-start.5 = (bf16[128,512]{1,0:T(8,128)(2,1)S(1)}, bf16[128,512]{1,0:T(8,128)(2,1)S(1)}, u32[]{:S(2)}, u32[]{:S(2)}) collective-permute-start(bf16[128,512]{1,0:T(8,128)(2,1)S(1)} %collective-permute-done.1.refs_5_), channel_id=1, source_target_pairs={{4,8},{6,10},{8,12},{10,14},{5,9},{7,11},{9,13},{11,15},{20,24},{2... | collective-permute-start | bytes 393224 | tf_op jit(solution)/shard_map/ppermute | solution.py:145
  10.8 10.0 %collective-permute-start.8 = (bf16[128,512]{1,0:T(8,128)(2,1)S(1)}, bf16[128,512]{1,0:T(8,128)(2,1)S(1)}, u32[]{:S(2)}, u32[]{:S(2)}) collective-permute-start(bf16[128,512]{1,0:T(8,128)(2,1)S(1)} %collective-permute-done.3.refs_8_), channel_id=1, source_target_pairs={{4,8},{6,10},{8,12},{10,14},{5,9},{7,11},{9,13},{11,15},{20,24},{2... | collective-permute-start | bytes 393224 | tf_op jit(solution)/shard_map/ppermute | solution.py:145
  12.1 10.1 %collective-permute-start.2 = (bf16[128,512]{1,0:T(8,128)(2,1)}, bf16[128,512]{1,0:T(8,128)(2,1)S(1)}, u32[]{:S(2)}, u32[]{:S(2)}) collective-permute-start(bf16[128,512]{1,0:T(8,128)(2,1)} %refs_6_.1), channel_id=1, source_target_pairs={{0,2},{2,0},{4,6},{6,4},{8,10},{10,8},{12,14},{14,12},{1,3},{3,1},... | collective-permute-start | bytes 393224 | tf_op jit(solution)/shard_map/ppermute | solution.py:153
  13.7 10.9 %collective-permute-start.4 = (bf16[128,512]{1,0:T(8,128)(2,1)S(1)}, bf16[128,512]{1,0:T(8,128)(2,1)S(1)}, u32[]{:S(2)}, u32[]{:S(2)}) collective-permute-start(bf16[128,512]{1,0:T(8,128)(2,1)S(1)} %collective-permute-done.1.refs_5_), channel_id=1, source_target_pairs={{4,6},{6,4},{8,10},{10,8},{12,14},{14,12},{5,7},{7,5},{9,11},{11,9... | collective-permute-start | bytes 393224 | tf_op jit(solution)/shard_map/ppermute | solution.py:153
  16.1 26.8 %collective-permute-start.7 = (bf16[128,512]{1,0:T(8,128)(2,1)S(1)}, bf16[128,512]{1,0:T(8,128)(2,1)S(1)}, u32[]{:S(2)}, u32[]{:S(2)}) collective-permute-start(bf16[128,512]{1,0:T(8,128)(2,1)S(1)} %collective-permute-done.3.refs_8_), channel_id=1, source_target_pairs={{4,6},{6,4},{8,10},{10,8},{12,14},{14,12},{5,7},{7,5},{9,11},{11,9... | collective-permute-start | bytes 393224 | tf_op jit(solution)/shard_map/ppermute | solution.py:153
  19.5 17.4 %collective-permute-start.10 = (bf16[128,512]{1,0:T(8,128)(2,1)S(1)}, bf16[128,512]{1,0:T(8,128)(2,1)S(1)}, u32[]{:S(2)}, u32[]{:S(2)}) collective-permute-start(bf16[128,512]{1,0:T(8,128)(2,1)S(1)} %collective-permute-done.5.refs_6_), channel_id=1, source_target_pairs={{8,12},{10,14},{9,13},{11,15},{24,28},{26,30},{25,29},{27,31}} | collective-permute-start | bytes 393224 | tf_op jit(solution)/shard_map/ppermute | solution.py:145
  20.8 18.6 %collective-permute-start.11 = (bf16[128,512]{1,0:T(8,128)(2,1)S(1)}, bf16[128,512]{1,0:T(8,128)(2,1)S(1)}, u32[]{:S(2)}, u32[]{:S(2)}) collective-permute-start(bf16[128,512]{1,0:T(8,128)(2,1)S(1)} %collective-permute-done.8.refs_9_), channel_id=1, source_target_pairs={{8,12},{10,14},{9,13},{11,15},{24,28},{26,30},{25,29},{27,31}} | collective-permute-start | bytes 393224 | tf_op jit(solution)/shard_map/ppermute | solution.py:145
  22.1 20.7 %collective-permute-start.6 = (bf16[128,512]{1,0:T(8,128)(2,1)S(1)}, bf16[128,512]{1,0:T(8,128)(2,1)S(1)}, u32[]{:S(2)}, u32[]{:S(2)}) collective-permute-start(bf16[128,512]{1,0:T(8,128)(2,1)S(1)} %collective-permute-done.5.refs_6_), channel_id=1, source_target_pairs={{8,10},{10,8},{12,14},{14,12},{9,11},{11,9},{13,15},{15,13},{24,26... | collective-permute-start | bytes 393224 | tf_op jit(solution)/shard_map/ppermute | solution.py:153
  24.6 18.3 %collective-permute-start.9 = (bf16[128,512]{1,0:T(8,128)(2,1)S(1)}, bf16[128,512]{1,0:T(8,128)(2,1)S(1)}, u32[]{:S(2)}, u32[]{:S(2)}) collective-permute-start(bf16[128,512]{1,0:T(8,128)(2,1)S(1)} %collective-permute-done.8.refs_9_), channel_id=1, source_target_pairs={{8,10},{10,8},{12,14},{14,12},{9,11},{11,9},{13,15},{15,13},{24,26... | collective-permute-start | bytes 393224 | tf_op jit(solution)/shard_map/ppermute | solution.py:153
  28.0 1.1 %copy-start = (bf16[128,3072]{1,0:T(8,128)(2,1)S(1)}, bf16[128,3072]{1,0:T(8,128)(2,1)}, u32[]{:S(2)}) copy-start(bf16[128,3072]{1,0:T(8,128)(2,1)} %refs_2_.7) | copy-start | bytes 2359300
  29.1 0.7 %copy-start.2 = (s32[4,4]{1,0:T(4,128)S(1)}, s32[4,4]{1,0:T(4,128)}, u32[]{:S(2)}) copy-start(s32[4,4]{1,0:T(4,128)} %refs_0_.7) | copy-start | bytes 196
  29.8 0.7 %copy-start.3 = (s32[4]{0:T(128)S(1)}, s32[4]{0:T(128)}, u32[]{:S(2)}) copy-start(s32[4]{0:T(128)} %refs_1_.7) | copy-start | bytes 52
  30.5 0.9 %copy-start.4 = (bf16[128,512]{1,0:T(8,128)(2,1)S(1)}, bf16[128,512]{1,0:T(8,128)(2,1)}, u32[]{:S(2)}) copy-start(bf16[128,512]{1,0:T(8,128)(2,1)} %refs_3_.2) | copy-start | bytes 393220
  31.4 0.9 %copy-start.5 = (bf16[128,512]{1,0:T(8,128)(2,1)S(1)}, bf16[128,512]{1,0:T(8,128)(2,1)}, u32[]{:S(2)}) copy-start(bf16[128,512]{1,0:T(8,128)(2,1)} %refs_6_.1) | copy-start | bytes 393220
  37.0 13.0 %collective-permute-start.12 = (bf16[128,512]{1,0:T(8,128)(2,1)S(1)}, bf16[128,512]{1,0:T(8,128)(2,1)S(1)}, u32[]{:S(2)}, u32[]{:S(2)}) collective-permute-start(bf16[128,512]{1,0:T(8,128)(2,1)S(1)} %collective-permute-done.10.refs_5_), channel_id=1, source_target_pairs={{12,14},{14,12},{13,15},{15,13},{28,30},{30,28},{29,31},{31,29}} | collective-permute-start | bytes 393224 | tf_op jit(solution)/shard_map/ppermute | solution.py:153
  39.4 10.5 %collective-permute-start.13 = (bf16[128,512]{1,0:T(8,128)(2,1)S(1)}, bf16[128,512]{1,0:T(8,128)(2,1)S(1)}, u32[]{:S(2)}, u32[]{:S(2)}) collective-permute-start(bf16[128,512]{1,0:T(8,128)(2,1)S(1)} %collective-permute-done.11.refs_6_), channel_id=1, source_target_pairs={{12,14},{14,12},{13,15},{15,13},{28,30},{30,28},{29,31},{31,29}} | collective-permute-start | bytes 393224 | tf_op jit(solution)/shard_map/ppermute | solution.py:153
  47.8 2.1 %copy-start.1 = (f32[4,3072]{1,0:T(4,128)S(1)}, f32[4,3072]{1,0:T(4,128)}, u32[]{:S(2)}) copy-start(f32[4,3072]{1,0:T(4,128)} %refs_3_.3) | copy-start | bytes 147460

commit v2 on v1

v2 whole, which is shorter than its diff:
```python
import math

import jax
import jax.numpy as jnp
from jax import lax
from jax.experimental import pallas as pl
from jax.experimental.pallas import tpu as pltpu
from jax.sharding import PartitionSpec as P

HEAD_SIZE = 128
CH = 256
LOG2E = math.log2(math.e)
LN2 = math.log(2.0)
FAR = 1e30


def attend_kernel(distances, per_span, first, last, refs_in, refs_out):
    refs = list(refs_in)
    mask_ref, section_ref, q_ref = refs[:3]
    refs = refs[3:]
    if last:
        gate_ref = refs.pop(0)
    if not first:
        acc_in, stat_in = refs.pop(0), refs.pop(0)
    blocks = len(distances)
    key_refs, value_refs = refs[:blocks], refs[blocks:]
    if last:
        mixed_ref, log_ref = refs_out
    else:
        acc_out, stat_out = refs_out
    rows, heads = q_ref.shape[0], q_ref.shape[1] // HEAD_SIZE
    kv_heads = key_refs[0].shape[1] // HEAD_SIZE
    group = heads // kv_heads
    span = lax.axis_index("tm") // per_span
    scale = LOG2E / math.sqrt(HEAD_SIZE)
    seen = []
    for distance in distances:
        if distance == 0:
            seen.append(None)
        else:
            behind = jnp.maximum(span - distance, 0)
            seen.append(jnp.logical_and(span >= distance, mask_ref[span, behind] > 0))
    if last:
        gate_row = gate_ref[pl.ds(section_ref[span], 1), :]

    for h in range(kv_heads):
        inside = slice(h * HEAD_SIZE, (h + 1) * HEAD_SIZE)
        queries = jnp.concatenate(
            [q_ref[:, (h * group + g) * HEAD_SIZE : (h * group + g + 1) * HEAD_SIZE] for g in range(group)], axis=0
        )
        scores = [
            scale * lax.dot_general(k[:, inside], queries, (((1,), (1,)), ((), ())), preferred_element_type=jnp.float32)
            for k in key_refs
        ]
        old = None if first else stat_in[h, 0:1, :]
        top = old
        for score, see in zip(scores, seen):
            row = jnp.max(score, axis=0, keepdims=True)
            if see is not None:
                row = jnp.where(see, row, -FAR)
            top = row if top is None else jnp.maximum(top, row)
        weights = [
            jnp.exp2(score - (top if see is None else jnp.where(see, top, FAR))) for score, see in zip(scores, seen)
        ]
        total = sum(jnp.sum(weight, axis=0, keepdims=True) for weight in weights)
        attended = lax.dot_general(
            jnp.concatenate([v[:, inside] for v in value_refs], axis=0),
            jnp.concatenate([weight.astype(jnp.bfloat16) for weight in weights], axis=0),
            (((0,), (0,)), ((), ())),
            preferred_element_type=jnp.float32,
        )
        if not first:
            factor = jnp.exp2(old - top)
            total += stat_in[h, 1:2, :] * factor
            attended += acc_in[h] * factor
        if not last:
            stat_out[h, 0:1, :] = top
            stat_out[h, 1:2, :] = total
            acc_out[h] = attended
            continue
        log_total = top * LN2 + jnp.log(total)
        attended = attended * (1.0 / total)
        for g in range(group):
            head = h * group + g
            columns = slice(head * HEAD_SIZE, (head + 1) * HEAD_SIZE)
            block = attended[:, g * rows : (g + 1) * rows].T
            mixed_ref[:, columns] = (gate_row[:, columns] * block).astype(jnp.bfloat16)
            log_ref[head : head + 1, :] = log_total[:, g * rows : (g + 1) * rows]


def attend(name, blocks, per_span, state, last, mask, section, queries, gate):
    rows, width = queries.shape
    heads = width // HEAD_SIZE
    kv_heads = blocks[0][1].shape[1] // HEAD_SIZE
    group = heads // kv_heads
    first = state is None
    operands = [mask, section, queries]
    specs = [pl.BlockSpec(memory_space=pltpu.SMEM)] * 2
    if last:
        operands.append(gate)
    if not first:
        operands += list(state)
    operands += [k for _, k, _ in blocks] + [v for _, _, v in blocks]
    specs += [pl.BlockSpec(memory_space=pltpu.VMEM)] * (len(operands) - len(specs))
    if last:
        out_shape = (
            jax.ShapeDtypeStruct((rows, width), jnp.bfloat16),
            jax.ShapeDtypeStruct((heads, rows), jnp.float32),
        )
    else:
        out_shape = (
            jax.ShapeDtypeStruct((kv_heads, HEAD_SIZE, group * rows), jnp.float32),
            jax.ShapeDtypeStruct((kv_heads, 8, group * rows), jnp.float32),
        )
    count = len(operands)

    def kernel(*refs):
        attend_kernel([d for d, _, _ in blocks], per_span, first, last, refs[:count], refs[count:])

    keys_seen = len(blocks) * rows
    return pl.pallas_call(
        kernel,
        out_shape=out_shape,
        in_specs=specs,
        out_specs=(pl.BlockSpec(memory_space=pltpu.VMEM),) * 2,
        compiler_params=pltpu.CompilerParams(vmem_limit_bytes=24 * 1024 * 1024),
        cost_estimate=pl.CostEstimate(
            flops=8 * keys_seen * rows * width,
            bytes_accessed=rows * width * 8,
            transcendentals=keys_seen * rows * heads,
        ),
        name=name,
    )(*operands)


def on_device(queries, keys, values, span_mask, section, section_gate):
    rows = queries.shape[0]
    count = lax.axis_size("tm")
    per_span = CH // rows
    spans = count // per_span

    def onward(value):
        return lax.ppermute(value, "tm", [(i, (i + per_span) % count) for i in range(count)])

    def around(value, turn):
        pairs = [(i, i - i % per_span + (i + turn) % per_span) for i in range(count)]
        return lax.ppermute(value, "tm", pairs)

    held = (keys, values)
    waiting = [(0, keys, values)]
    state = None
    for distance in range(spans + 1):
        coming = []
        if distance < spans:
            for turn in range(1, per_span):
                coming.append((distance,) + tuple(around(x, turn) for x in held))
        if distance + 1 < spans:
            held = tuple(onward(x) for x in held)
            coming.append((distance + 1,) + held)
        last = distance == spans
        state = attend(
            "attend_%d" % distance, waiting, per_span, state, last, span_mask, section, queries, section_gate
        )
        if not last:
            held, state = lax.optimization_barrier((held, state))
            if distance + 1 < spans:
                coming[-1] = (distance + 1,) + held
        waiting = coming
    return state


def solution(mesh):
    placed = (
        P(("grp", "tm"), "head"),
        P(("grp", "tm"), "head"),
        P(("grp", "tm"), "head"),
        P("grp", None),
        P("grp"),
        P(None, "head"),
    )
    return jax.shard_map(
        on_device,
        mesh=mesh,
        in_specs=placed,
        out_specs=(P(("grp", "tm"), "head"), P("head", ("grp", "tm"))),
        check_vma=False,
    )
```

time: 53.9 us -> 40.2 us (0.75)
  the two profiles are of different devices: /device:TPU:24 before, /device:TPU:0 now
where the time goes in v2:
time: 40.2 us; the launch traced here: 40 us
  starting transfers between devices  15.3 us (38%)
  Pallas kernels  12.3 us (31%)
  waiting for transfers between devices  7.45 us (19%)
  local copies, waits for them, and re-layouts  4.28 us (11%)
  between operations  0.7 us (2%)
    pallas_call x5, Pallas kernels, attend(): pl.pallas_call(kernel, out_shape=out_shape, in_specs=specs, out_specs=(pl...  12.3 us
    ppermute x8, starting transfers between devices, around(): return lax.ppermute(value, 'tm', pairs)  8.1 us
    ppermute x6, starting transfers between devices, onward(): lax.ppermute(value, 'tm', [(i, (i + per_span) % count) for i in range(cou...  7.15 us
    ppermute x6, waiting for transfers between devices, onward(): lax.ppermute(value, 'tm', [(i, (i + per_span) % count) for i in range(cou...  5.44 us
    unnamed x12, local copies, waits for them, and re-layouts  4.28 us
    ppermute x8, waiting for transfers between devices, around(): return lax.ppermute(value, 'tm', pairs)  2.01 us
  transfers between devices with their start and end apart: 14, of which 6 were waited for; matrix products, arithmetic and copies ran while one was open for 0% of the time, Pallas kernels for 23%

profile of v2, /device:TPU:0, one launch (start us, length us, event | category | flops | bytes accessed | tf_op | source)
XLA Modules:
  0.0 40.0 jit_solution(11986319014056242724)
XLA Ops:
  0.6 3.1 %collective-permute-start = (bf16[128,512]{1,0:T(8,128)(2,1)}, bf16[128,512]{1,0:T(8,128)(2,1)S(1)}, u32[]{:S(2)}, u32[]{:S(2)}) collective-permute-start(bf16[128,512]{1,0:T(8,128)(2,1)} %refs_3_.2), channel_id=1, source_target_pairs={{0,4},{2,6},{4,8},{6,10},{8,12},{10,14},{12,0},{14,2},{1,5},{3,7},... | collective-permute-start | bytes 393224 | tf_op jit(solution)/shard_map/ppermute | solution.py:143
  3.7 1.6 %collective-permute-start.1 = (bf16[128,512]{1,0:T(8,128)(2,1)}, bf16[128,512]{1,0:T(8,128)(2,1)S(1)}, u32[]{:S(2)}, u32[]{:S(2)}) collective-permute-start(bf16[128,512]{1,0:T(8,128)(2,1)} %refs_4_.1), channel_id=1, source_target_pairs={{0,4},{2,6},{4,8},{6,10},{8,12},{10,14},{12,0},{14,2},{1,5},{3,7},... | collective-permute-start | bytes 393224 | tf_op jit(solution)/shard_map/ppermute | solution.py:143
  5.3 1.5 %collective-permute-start.4 = (bf16[128,512]{1,0:T(8,128)(2,1)}, bf16[128,512]{1,0:T(8,128)(2,1)S(1)}, u32[]{:S(2)}, u32[]{:S(2)}) collective-permute-start(bf16[128,512]{1,0:T(8,128)(2,1)} %refs_3_.2), channel_id=1, source_target_pairs={{0,2},{2,0},{4,6},{6,4},{8,10},{10,8},{12,14},{14,12},{1,3},{3,1},... | collective-permute-start | bytes 393224 | tf_op jit(solution)/shard_map/ppermute | solution.py:147
  6.8 0.5 %collective-permute-start.5 = (bf16[128,512]{1,0:T(8,128)(2,1)}, bf16[128,512]{1,0:T(8,128)(2,1)S(1)}, u32[]{:S(2)}, u32[]{:S(2)}) collective-permute-start(bf16[128,512]{1,0:T(8,128)(2,1)} %refs_4_.1), channel_id=1, source_target_pairs={{0,2},{2,0},{4,6},{6,4},{8,10},{10,8},{12,14},{14,12},{1,3},{3,1},... | collective-permute-start | bytes 393224 | tf_op jit(solution)/shard_map/ppermute | solution.py:147
  7.3 0.0 copy-start
  7.3 1.1 %copy-done = bf16[128,3072]{1,0:T(8,128)(2,1)S(1)} copy-done((bf16[128,3072]{1,0:T(8,128)(2,1)S(1)}, bf16[128,3072]{1,0:T(8,128)(2,1)}, u32[]{:S(2)}) %copy-start) | copy-done | bytes 786456
  8.4 0.0 copy-start.2
  8.4 0.7 %copy-done.2 = s32[4,4]{1,0:T(4,128)S(1)} copy-done((s32[4,4]{1,0:T(4,128)S(1)}, s32[4,4]{1,0:T(4,128)}, u32[]{:S(2)}) %copy-start.2) | copy-done | bytes 88
  9.1 0.0 copy-start.3
  9.1 0.7 %copy-done.3 = s32[4]{0:T(128)S(1)} copy-done((s32[4]{0:T(128)S(1)}, s32[4]{0:T(128)}, u32[]{:S(2)}) %copy-start.3) | copy-done | bytes 40
  9.8 0.0 copy-start.4
  9.8 0.9 %copy-done.4 = bf16[128,512]{1,0:T(8,128)(2,1)S(1)} copy-done((bf16[128,512]{1,0:T(8,128)(2,1)S(1)}, bf16[128,512]{1,0:T(8,128)(2,1)}, u32[]{:S(2)}) %copy-start.4) | copy-done | bytes 131096
  10.7 0.0 copy-start.5
  10.7 0.9 %copy-done.5 = bf16[128,512]{1,0:T(8,128)(2,1)S(1)} copy-done((bf16[128,512]{1,0:T(8,128)(2,1)S(1)}, bf16[128,512]{1,0:T(8,128)(2,1)}, u32[]{:S(2)}) %copy-start.5) | copy-done | bytes 131096
  11.6 1.9 %attend_0.1 = (f32[4,128,768]{2,1,0:T(8,128)S(1)}, f32[4,8,768]{2,1,0:T(8,128)S(1)}) custom-call(s32[4,4]{1,0:T(4,128)S(1)} %copy-done.2, s32[4]{0:T(128)S(1)} %copy-done.3, bf16[128,3072]{1,0:T(8,128)(2,1)S(1)} %copy-done, bf16[128,512]{1,0:T(8,128)(2,1)S(1)} %copy-done.4, bf16[128,512]{1,0:T(8,128)(2,1)S(1)} %copy-done.5), custom_call_target="tpu_custom_call" | custom-call | flops 402653184 | bytes 3145728 | tf_op jit(solution)/shard_map/attend_0/pallas_call | solution.py:121
  13.5 0.0 collective-permute-done.refs_6_
  13.5 0.0 collective-permute-done.1.refs_8_
  13.5 1.6 %collective-permute-start.2 = (bf16[128,512]{1,0:T(8,128)(2,1)S(1)}, bf16[128,512]{1,0:T(8,128)(2,1)S(1)}, u32[]{:S(2)}, u32[]{:S(2)}) collective-permute-start(bf16[128,512]{1,0:T(8,128)(2,1)S(1)} %collective-permute-done.refs_6_), channel_id=1, source_target_pairs={{0,4},{2,6},{4,8},{6,10},{8,12},{10,14},{12,0},{14,2},{1,5},{3,7},... | collective-permute-start | bytes 393224 | tf_op jit(solution)/shard_map/ppermute | solution.py:143
  15.1 0.1 collective-permute-start.3
  15.2 1.7 %collective-permute-start.8 = (bf16[128,512]{1,0:T(8,128)(2,1)S(1)}, bf16[128,512]{1,0:T(8,128)(2,1)S(1)}, u32[]{:S(2)}, u32[]{:S(2)}) collective-permute-start(bf16[128,512]{1,0:T(8,128)(2,1)S(1)} %collective-permute-done.refs_6_), channel_id=1, source_target_pairs={{0,2},{2,0},{4,6},{6,4},{8,10},{10,8},{12,14},{14,12},{1,3},{3,1},... | collective-permute-start | bytes 393224 | tf_op jit(solution)/shard_map/ppermute | solution.py:147
  16.9 0.0 collective-permute-done.4.refs_5_
  16.9 0.3 collective-permute-start.9
  17.2 0.0 collective-permute-done.5.refs_7_
  17.2 2.5 %attend_1.1 = (f32[4,128,768]{2,1,0:T(8,128)S(1)}, f32[4,8,768]{2,1,0:T(8,128)S(1)}) custom-call(s32[4,4]{1,0:T(4,128)S(1)} %copy-done.2, s32[4]{0:T(128)S(1)} %copy-done.3, bf16[128,3072]{1,0:T(8,128)(2,1)S(1)} %copy-done, f32[4,128,768]{2,1,0:T(8,128)S(1)} %get-tuple-element.28.refs_3_, f32[4,8,768]{2,1,0:T(8,128)S(1)} %get-tuple-element.29.refs_4_, ...), custom_call_target="tpu_custom_call" | custom-call | flops 805306368 | bytes 3145728 | tf_op jit(solution)/shard_map/attend_1/pallas_call | solution.py:121
  19.7 1.2 %collective-permute-done.2.refs_6_ = bf16[128,512]{1,0:T(8,128)(2,1)S(1)} collective-permute-done((bf16[128,512]{1,0:T(8,128)(2,1)S(1)}, bf16[128,512]{1,0:T(8,128)(2,1)S(1)}, u32[]{:S(2)}, u32[]{:S(2)}) %collective-permute-start.2) | collective-permute-done | bytes 131104 | tf_op jit(solution)/shard_map/ppermute | solution.py:143
  20.8 1.4 %collective-permute-done.3.refs_8_ = bf16[128,512]{1,0:T(8,128)(2,1)S(1)} collective-permute-done((bf16[128,512]{1,0:T(8,128)(2,1)S(1)}, bf16[128,512]{1,0:T(8,128)(2,1)S(1)}, u32[]{:S(2)}, u32[]{:S(2)}) %collective-permute-start.3) | collective-permute-done | bytes 131104 | tf_op jit(solution)/shard_map/ppermute | solution.py:143
  22.3 0.0 collective-permute-start.6
  22.3 0.8 %collective-permute-start.7 = (bf16[128,512]{1,0:T(8,128)(2,1)S(1)}, bf16[128,512]{1,0:T(8,128)(2,1)S(1)}, u32[]{:S(2)}, u32[]{:S(2)}) collective-permute-start(bf16[128,512]{1,0:T(8,128)(2,1)S(1)} %collective-permute-done.3.refs_8_), channel_id=1, source_target_pairs={{0,4},{2,6},{4,8},{6,10},{8,12},{10,14},{12,0},{14,2},{1,5},{3,7},... | collective-permute-start | bytes 393224 | tf_op jit(solution)/shard_map/ppermute | solution.py:143
  23.1 1.5 %collective-permute-start.10 = (bf16[128,512]{1,0:T(8,128)(2,1)S(1)}, bf16[128,512]{1,0:T(8,128)(2,1)S(1)}, u32[]{:S(2)}, u32[]{:S(2)}) collective-permute-start(bf16[128,512]{1,0:T(8,128)(2,1)S(1)} %collective-permute-done.2.refs_6_), channel_id=1, source_target_pairs={{0,2},{2,0},{4,6},{6,4},{8,10},{10,8},{12,14},{14,12},{1,3},{3,1},... | collective-permute-start | bytes 393224 | tf_op jit(solution)/shard_map/ppermute | solution.py:147
  24.6 0.0 collective-permute-done.8.refs_5_
  24.6 0.5 %collective-permute-start.11 = (bf16[128,512]{1,0:T(8,128)(2,1)S(1)}, bf16[128,512]{1,0:T(8,128)(2,1)S(1)}, u32[]{:S(2)}, u32[]{:S(2)}) collective-permute-start(bf16[128,512]{1,0:T(8,128)(2,1)S(1)} %collective-permute-done.3.refs_8_), channel_id=1, source_target_pairs={{0,2},{2,0},{4,6},{6,4},{8,10},{10,8},{12,14},{14,12},{1,3},{3,1},... | collective-permute-start | bytes 393224 | tf_op jit(solution)/shard_map/ppermute | solution.py:147
  25.1 0.0 collective-permute-done.9.refs_7_
  25.1 2.5 %attend_2.1 = (f32[4,128,768]{2,1,0:T(8,128)S(1)}, f32[4,8,768]{2,1,0:T(8,128)S(1)}) custom-call(s32[4,4]{1,0:T(4,128)S(1)} %copy-done.2, s32[4]{0:T(128)S(1)} %copy-done.3, bf16[128,3072]{1,0:T(8,128)(2,1)S(1)} %copy-done, f32[4,128,768]{2,1,0:T(8,128)S(1)} %get-tuple-element.34.refs_3_, f32[4,8,768]{2,1,0:T(8,128)S(1)} %get-tuple-element.35.refs_4_, ...), custom_call_target="tpu_custom_call" | custom-call | flops 805306368 | bytes 3145728 | tf_op jit(solution)/shard_map/attend_2/pallas_call | solution.py:121
  27.6 0.0 copy-start.1
  27.6 1.4 %collective-permute-done.6.refs_6_ = bf16[128,512]{1,0:T(8,128)(2,1)S(1)} collective-permute-done((bf16[128,512]{1,0:T(8,128)(2,1)S(1)}, bf16[128,512]{1,0:T(8,128)(2,1)S(1)}, u32[]{:S(2)}, u32[]{:S(2)}) %collective-permute-start.6) | collective-permute-done | bytes 131104 | tf_op jit(solution)/shard_map/ppermute | solution.py:143
  29.0 1.4 %collective-permute-done.7.refs_8_ = bf16[128,512]{1,0:T(8,128)(2,1)S(1)} collective-permute-done((bf16[128,512]{1,0:T(8,128)(2,1)S(1)}, bf16[128,512]{1,0:T(8,128)(2,1)S(1)}, u32[]{:S(2)}, u32[]{:S(2)}) %collective-permute-start.7) | collective-permute-done | bytes 131104 | tf_op jit(solution)/shard_map/ppermute | solution.py:143
  30.4 1.5 %collective-permute-start.12 = (bf16[128,512]{1,0:T(8,128)(2,1)S(1)}, bf16[128,512]{1,0:T(8,128)(2,1)S(1)}, u32[]{:S(2)}, u32[]{:S(2)}) collective-permute-start(bf16[128,512]{1,0:T(8,128)(2,1)S(1)} %collective-permute-done.6.refs_6_), channel_id=1, source_target_pairs={{0,2},{2,0},{4,6},{6,4},{8,10},{10,8},{12,14},{14,12},{1,3},{3,1},... | collective-permute-start | bytes 393224 | tf_op jit(solution)/shard_map/ppermute | solution.py:147
  32.0 0.5 %collective-permute-start.13 = (bf16[128,512]{1,0:T(8,128)(2,1)S(1)}, bf16[128,512]{1,0:T(8,128)(2,1)S(1)}, u32[]{:S(2)}, u32[]{:S(2)}) collective-permute-start(bf16[128,512]{1,0:T(8,128)(2,1)S(1)} %collective-permute-done.7.refs_8_), channel_id=1, source_target_pairs={{0,2},{2,0},{4,6},{6,4},{8,10},{10,8},{12,14},{14,12},{1,3},{3,1},... | collective-permute-start | bytes 393224 | tf_op jit(solution)/shard_map/ppermute | solution.py:147
  32.5 0.0 collective-permute-done.10.refs_5_
  32.5 0.0 collective-permute-done.11.refs_7_
  32.5 2.5 %attend_3.1 = (f32[4,128,768]{2,1,0:T(8,128)S(1)}, f32[4,8,768]{2,1,0:T(8,128)S(1)}) custom-call(s32[4,4]{1,0:T(4,128)S(1)} %copy-done.2, s32[4]{0:T(128)S(1)} %copy-done.3, bf16[128,3072]{1,0:T(8,128)(2,1)S(1)} %copy-done, f32[4,128,768]{2,1,0:T(8,128)S(1)} %get-tuple-element.40.refs_3_, f32[4,8,768]{2,1,0:T(8,128)S(1)} %get-tuple-element.41.refs_4_, ...), custom_call_target="tpu_custom_call" | custom-call | flops 805306368 | bytes 3145728 | tf_op jit(solution)/shard_map/attend_3/pallas_call | solution.py:121
  34.9 0.5 %collective-permute-done.12.refs_6_ = bf16[128,512]{1,0:T(8,128)(2,1)S(1)} collective-permute-done((bf16[128,512]{1,0:T(8,128)(2,1)S(1)}, bf16[128,512]{1,0:T(8,128)(2,1)S(1)}, u32[]{:S(2)}, u32[]{:S(2)}) %collective-permute-start.12) | collective-permute-done | bytes 131104 | tf_op jit(solution)/shard_map/ppermute | solution.py:147
  35.4 1.5 %collective-permute-done.13.refs_7_ = bf16[128,512]{1,0:T(8,128)(2,1)S(1)} collective-permute-done((bf16[128,512]{1,0:T(8,128)(2,1)S(1)}, bf16[128,512]{1,0:T(8,128)(2,1)S(1)}, u32[]{:S(2)}, u32[]{:S(2)}) %collective-permute-start.13) | collective-permute-done | bytes 131104 | tf_op jit(solution)/shard_map/ppermute | solution.py:147
  36.9 0.0 copy-done.1
  36.9 3.0 %attend_4.1 = (bf16[128,3072]{1,0:T(8,128)(2,1)}, f32[24,128]{1,0:T(8,128)}) custom-call(s32[4,4]{1,0:T(4,128)S(1)} %copy-done.2, s32[4]{0:T(128)S(1)} %copy-done.3, bf16[128,3072]{1,0:T(8,128)(2,1)S(1)} %copy-done, f32[4,3072]{1,0:T(4,128)S(1)} %copy-done.1, f32[4,128,768]{2,1,0:T(8,128)S(1)} %get-tuple-element.44.refs_4_, ...), custom_call_target="tpu_custom_call" | custom-call | flops 402653184 | bytes 3145728 | tf_op jit(solution)/shard_map/attend_4/pallas_call | solution.py:121
Async XLA Ops:
  0.6 12.8 %collective-permute-start = (bf16[128,512]{1,0:T(8,128)(2,1)}, bf16[128,512]{1,0:T(8,128)(2,1)S(1)}, u32[]{:S(2)}, u32[]{:S(2)}) collective-permute-start(bf16[128,512]{1,0:T(8,128)(2,1)} %refs_3_.2), channel_id=1, source_target_pairs={{0,4},{2,6},{4,8},{6,10},{8,12},{10,14},{12,0},{14,2},{1,5},{3,7},... | collective-permute-start | bytes 393224 | tf_op jit(solution)/shard_map/ppermute | solution.py:143
  3.7 9.8 %collective-permute-start.1 = (bf16[128,512]{1,0:T(8,128)(2,1)}, bf16[128,512]{1,0:T(8,128)(2,1)S(1)}, u32[]{:S(2)}, u32[]{:S(2)}) collective-permute-start(bf16[128,512]{1,0:T(8,128)(2,1)} %refs_4_.1), channel_id=1, source_target_pairs={{0,4},{2,6},{4,8},{6,10},{8,12},{10,14},{12,0},{14,2},{1,5},{3,7},... | collective-permute-start | bytes 393224 | tf_op jit(solution)/shard_map/ppermute | solution.py:143
  5.3 11.6 %collective-permute-start.4 = (bf16[128,512]{1,0:T(8,128)(2,1)}, bf16[128,512]{1,0:T(8,128)(2,1)S(1)}, u32[]{:S(2)}, u32[]{:S(2)}) collective-permute-start(bf16[128,512]{1,0:T(8,128)(2,1)} %refs_3_.2), channel_id=1, source_target_pairs={{0,2},{2,0},{4,6},{6,4},{8,10},{10,8},{12,14},{14,12},{1,3},{3,1},... | collective-permute-start | bytes 393224 | tf_op jit(solution)/shard_map/ppermute | solution.py:147
  6.8 10.4 %collective-permute-start.5 = (bf16[128,512]{1,0:T(8,128)(2,1)}, bf16[128,512]{1,0:T(8,128)(2,1)S(1)}, u32[]{:S(2)}, u32[]{:S(2)}) collective-permute-start(bf16[128,512]{1,0:T(8,128)(2,1)} %refs_4_.1), channel_id=1, source_target_pairs={{0,2},{2,0},{4,6},{6,4},{8,10},{10,8},{12,14},{14,12},{1,3},{3,1},... | collective-permute-start | bytes 393224 | tf_op jit(solution)/shard_map/ppermute | solution.py:147
  7.3 1.1 %copy-start = (bf16[128,3072]{1,0:T(8,128)(2,1)S(1)}, bf16[128,3072]{1,0:T(8,128)(2,1)}, u32[]{:S(2)}) copy-start(bf16[128,3072]{1,0:T(8,128)(2,1)} %refs_2_.9) | copy-start | bytes 2359300
  8.4 0.7 %copy-start.2 = (s32[4,4]{1,0:T(4,128)S(1)}, s32[4,4]{1,0:T(4,128)}, u32[]{:S(2)}) copy-start(s32[4,4]{1,0:T(4,128)} %refs_0_.9) | copy-start | bytes 196
  9.1 0.7 %copy-start.3 = (s32[4]{0:T(128)S(1)}, s32[4]{0:T(128)}, u32[]{:S(2)}) copy-start(s32[4]{0:T(128)} %refs_1_.9) | copy-start | bytes 52
  9.8 0.9 %copy-start.4 = (bf16[128,512]{1,0:T(8,128)(2,1)S(1)}, bf16[128,512]{1,0:T(8,128)(2,1)}, u32[]{:S(2)}) copy-start(bf16[128,512]{1,0:T(8,128)(2,1)} %refs_3_.2) | copy-start | bytes 393220
  10.7 0.9 %copy-start.5 = (bf16[128,512]{1,0:T(8,128)(2,1)S(1)}, bf16[128,512]{1,0:T(8,128)(2,1)}, u32[]{:S(2)}) copy-start(bf16[128,512]{1,0:T(8,128)(2,1)} %refs_4_.1) | copy-start | bytes 393220
  13.5 7.4 %collective-permute-start.2 = (bf16[128,512]{1,0:T(8,128)(2,1)S(1)}, bf16[128,512]{1,0:T(8,128)(2,1)S(1)}, u32[]{:S(2)}, u32[]{:S(2)}) collective-permute-start(bf16[128,512]{1,0:T(8,128)(2,1)S(1)} %collective-permute-done.refs_6_), channel_id=1, source_target_pairs={{0,4},{2,6},{4,8},{6,10},{8,12},{10,14},{12,0},{14,2},{1,5},{3,7},... | collective-permute-start | bytes 393224 | tf_op jit(solution)/shard_map/ppermute | solution.py:143
  15.1 7.1 %collective-permute-start.3 = (bf16[128,512]{1,0:T(8,128)(2,1)S(1)}, bf16[128,512]{1,0:T(8,128)(2,1)S(1)}, u32[]{:S(2)}, u32[]{:S(2)}) collective-permute-start(bf16[128,512]{1,0:T(8,128)(2,1)S(1)} %collective-permute-done.1.refs_8_), channel_id=1, source_target_pairs={{0,4},{2,6},{4,8},{6,10},{8,12},{10,14},{12,0},{14,2},{1,5},{3,7},... | collective-permute-start | bytes 393224 | tf_op jit(solution)/shard_map/ppermute | solution.py:143
  15.2 9.4 %collective-permute-start.8 = (bf16[128,512]{1,0:T(8,128)(2,1)S(1)}, bf16[128,512]{1,0:T(8,128)(2,1)S(1)}, u32[]{:S(2)}, u32[]{:S(2)}) collective-permute-start(bf16[128,512]{1,0:T(8,128)(2,1)S(1)} %collective-permute-done.refs_6_), channel_id=1, source_target_pairs={{0,2},{2,0},{4,6},{6,4},{8,10},{10,8},{12,14},{14,12},{1,3},{3,1},... | collective-permute-start | bytes 393224 | tf_op jit(solution)/shard_map/ppermute | solution.py:147
  16.9 8.2 %collective-permute-start.9 = (bf16[128,512]{1,0:T(8,128)(2,1)S(1)}, bf16[128,512]{1,0:T(8,128)(2,1)S(1)}, u32[]{:S(2)}, u32[]{:S(2)}) collective-permute-start(bf16[128,512]{1,0:T(8,128)(2,1)S(1)} %collective-permute-done.1.refs_8_), channel_id=1, source_target_pairs={{0,2},{2,0},{4,6},{6,4},{8,10},{10,8},{12,14},{14,12},{1,3},{3,1},... | collective-permute-start | bytes 393224 | tf_op jit(solution)/shard_map/ppermute | solution.py:147
  22.3 6.8 %collective-permute-start.6 = (bf16[128,512]{1,0:T(8,128)(2,1)S(1)}, bf16[128,512]{1,0:T(8,128)(2,1)S(1)}, u32[]{:S(2)}, u32[]{:S(2)}) collective-permute-start(bf16[128,512]{1,0:T(8,128)(2,1)S(1)} %collective-permute-done.2.refs_6_), channel_id=1, source_target_pairs={{0,4},{2,6},{4,8},{6,10},{8,12},{10,14},{12,0},{14,2},{1,5},{3,7},... | collective-permute-start | bytes 393224 | tf_op jit(solution)/shard_map/ppermute | solution.py:143
  22.3 8.2 %collective-permute-start.7 = (bf16[128,512]{1,0:T(8,128)(2,1)S(1)}, bf16[128,512]{1,0:T(8,128)(2,1)S(1)}, u32[]{:S(2)}, u32[]{:S(2)}) collective-permute-start(bf16[128,512]{1,0:T(8,128)(2,1)S(1)} %collective-permute-done.3.refs_8_), channel_id=1, source_target_pairs={{0,4},{2,6},{4,8},{6,10},{8,12},{10,14},{12,0},{14,2},{1,5},{3,7},... | collective-permute-start | bytes 393224 | tf_op jit(solution)/shard_map/ppermute | solution.py:143
  23.1 9.4 %collective-permute-start.10 = (bf16[128,512]{1,0:T(8,128)(2,1)S(1)}, bf16[128,512]{1,0:T(8,128)(2,1)S(1)}, u32[]{:S(2)}, u32[]{:S(2)}) collective-permute-start(bf16[128,512]{1,0:T(8,128)(2,1)S(1)} %collective-permute-done.2.refs_6_), channel_id=1, source_target_pairs={{0,2},{2,0},{4,6},{6,4},{8,10},{10,8},{12,14},{14,12},{1,3},{3,1},... | collective-permute-start | bytes 393224 | tf_op jit(solution)/shard_map/ppermute | solution.py:147
  24.6 7.9 %collective-permute-start.11 = (bf16[128,512]{1,0:T(8,128)(2,1)S(1)}, bf16[128,512]{1,0:T(8,128)(2,1)S(1)}, u32[]{:S(2)}, u32[]{:S(2)}) collective-permute-start(bf16[128,512]{1,0:T(8,128)(2,1)S(1)} %collective-permute-done.3.refs_8_), channel_id=1, source_target_pairs={{0,2},{2,0},{4,6},{6,4},{8,10},{10,8},{12,14},{14,12},{1,3},{3,1},... | collective-permute-start | bytes 393224 | tf_op jit(solution)/shard_map/ppermute | solution.py:147
  27.6 9.4 %copy-start.1 = (f32[4,3072]{1,0:T(4,128)S(1)}, f32[4,3072]{1,0:T(4,128)}, u32[]{:S(2)}) copy-start(f32[4,3072]{1,0:T(4,128)} %refs_3_.3) | copy-start | bytes 147460
  30.4 5.0 %collective-permute-start.12 = (bf16[128,512]{1,0:T(8,128)(2,1)S(1)}, bf16[128,512]{1,0:T(8,128)(2,1)S(1)}, u32[]{:S(2)}, u32[]{:S(2)}) collective-permute-start(bf16[128,512]{1,0:T(8,128)(2,1)S(1)} %collective-permute-done.6.refs_6_), channel_id=1, source_target_pairs={{0,2},{2,0},{4,6},{6,4},{8,10},{10,8},{12,14},{14,12},{1,3},{3,1},... | collective-permute-start | bytes 393224 | tf_op jit(solution)/shard_map/ppermute | solution.py:147
  32.0 5.0 %collective-permute-start.13 = (bf16[128,512]{1,0:T(8,128)(2,1)S(1)}, bf16[128,512]{1,0:T(8,128)(2,1)S(1)}, u32[]{:S(2)}, u32[]{:S(2)}) collective-permute-start(bf16[128,512]{1,0:T(8,128)(2,1)S(1)} %collective-permute-done.7.refs_8_), channel_id=1, source_target_pairs={{0,2},{2,0},{4,6},{6,4},{8,10},{10,8},{12,14},{14,12},{1,3},{3,1},... | collective-permute-start | bytes 393224 | tf_op jit(solution)/shard_map/ppermute | solution.py:147

commit v3 on v0

v3 whole, which is shorter than its diff:
```python
import math

import jax
import jax.numpy as jnp
from jax import lax
from jax.experimental import pallas as pl
from jax.experimental.pallas import tpu as pltpu
from jax.sharding import PartitionSpec as P

HEAD_SIZE = 128
CH = 256
LOG2E = math.log2(math.e)
LN2 = math.log(2.0)
FAR = 1e30


def weigh_kernel(per_span, mask_ref, q_ref, k_ref, weight_ref, inverse_ref, log_ref, score_ref):
    rows, heads = q_ref.shape[0], q_ref.shape[1] // HEAD_SIZE
    kv_heads = k_ref.shape[1] // HEAD_SIZE
    group = heads // kv_heads
    spans = k_ref.shape[0] // CH
    span = lax.axis_index("tm") // per_span
    scale = LOG2E / math.sqrt(HEAD_SIZE)
    seen = [jnp.logical_and(span >= s, mask_ref[span, s] > 0) for s in range(spans)]
    for h in range(kv_heads):
        inside = slice(h * HEAD_SIZE, (h + 1) * HEAD_SIZE)
        queries = jnp.concatenate(
            [q_ref[:, (h * group + g) * HEAD_SIZE : (h * group + g + 1) * HEAD_SIZE] for g in range(group)], axis=0
        )
        top = None
        for s in range(spans):
            score = scale * lax.dot_general(
                k_ref[s * CH : (s + 1) * CH, inside], queries, (((1,), (1,)), ((), ())),
                preferred_element_type=jnp.float32,
            )
            score_ref[h % 2, s] = score
            row = jnp.where(seen[s], jnp.max(score, axis=0, keepdims=True), -FAR)
            top = row if top is None else jnp.maximum(top, row)
        total = 0.0
        for s in range(spans):
            weight = jnp.exp2(score_ref[h % 2, s] - jnp.where(seen[s], top, FAR))
            total += jnp.sum(weight, axis=0, keepdims=True)
            weight_ref[h, s * CH : (s + 1) * CH, :] = weight.astype(jnp.bfloat16)
        inverse_ref[h, 0:1, :] = 1.0 / total
        log_total = top * LN2 + jnp.log(total)
        for g in range(group):
            log_ref[h * group + g : h * group + g + 1, :] = log_total[:, g * rows : (g + 1) * rows]


def mix_kernel(per_span, section_ref, weight_ref, inverse_ref, gate_ref, v_ref, mixed_ref):
    rows, heads = mixed_ref.shape[0], mixed_ref.shape[1] // HEAD_SIZE
    kv_heads = v_ref.shape[1] // HEAD_SIZE
    group = heads // kv_heads
    span = lax.axis_index("tm") // per_span
    gate_row = gate_ref[pl.ds(section_ref[span], 1), :]
    for h in range(kv_heads):
        attended = lax.dot_general(
            v_ref[:, h * HEAD_SIZE : (h + 1) * HEAD_SIZE], weight_ref[h], (((0,), (0,)), ((), ())),
            preferred_element_type=jnp.float32,
        )
        attended = attended * inverse_ref[h, 0:1, :]
        for g in range(group):
            columns = slice((h * group + g) * HEAD_SIZE, (h * group + g + 1) * HEAD_SIZE)
            block = attended[:, g * rows : (g + 1) * rows].T
            mixed_ref[:, columns] = (gate_row[:, columns] * block).astype(jnp.bfloat16)


def on_device(queries, keys, values, span_mask, section, section_gate):
    rows, width = queries.shape
    heads, kv_heads = width // HEAD_SIZE, keys.shape[1] // HEAD_SIZE
    group = heads // kv_heads
    per_span = CH // rows
    all_keys = lax.all_gather(keys, "tm", axis=0, tiled=True)
    all_values = lax.all_gather(values, "tm", axis=0, tiled=True)
    total = all_keys.shape[0]
    smem, vmem = pl.BlockSpec(memory_space=pltpu.SMEM), pl.BlockSpec(memory_space=pltpu.VMEM)
    params = pltpu.CompilerParams(vmem_limit_bytes=(24 if total <= 2048 else 56) * 1024 * 1024)
    score_bytes = total * group * rows * 4

    def weigh(*refs):
        weigh_kernel(per_span, *refs)

    def mix(*refs):
        mix_kernel(per_span, *refs)

    weight, inverse, log_total = pl.pallas_call(
        weigh,
        out_shape=(
            jax.ShapeDtypeStruct((kv_heads, total, group * rows), jnp.bfloat16),
            jax.ShapeDtypeStruct((kv_heads, 8, group * rows), jnp.float32),
            jax.ShapeDtypeStruct((heads, rows), jnp.float32),
        ),
        in_specs=[smem, vmem, vmem],
        out_specs=(vmem,) * 3,
        scratch_shapes=[pltpu.VMEM((2, total // CH, CH, group * rows), jnp.float32)],
        compiler_params=params,
        cost_estimate=pl.CostEstimate(
            flops=4 * total * rows * width, bytes_accessed=kv_heads * score_bytes // 2, transcendentals=kv_heads * score_bytes // 4
        ),
        name="weigh",
    )(span_mask, queries, all_keys)
    mixed = pl.pallas_call(
        mix,
        out_shape=jax.ShapeDtypeStruct((rows, width), jnp.bfloat16),
        in_specs=[smem] + [vmem] * 4,
        out_specs=vmem,
        compiler_params=params,
        cost_estimate=pl.CostEstimate(
            flops=4 * total * rows * width, bytes_accessed=kv_heads * score_bytes // 2, transcendentals=0
        ),
        name="mix",
    )(section, weight, inverse, section_gate, all_values)
    return mixed, log_total


def solution(mesh):
    placed = (
        P(("grp", "tm"), "head"),
        P(("grp", "tm"), "head"),
        P(("grp", "tm"), "head"),
        P("grp", None),
        P("grp"),
        P(None, "head"),
    )
    return jax.shard_map(
        on_device,
        mesh=mesh,
        in_specs=placed,
        out_specs=(P(("grp", "tm"), "head"), P("head", ("grp", "tm"))),
        check_vma=False,
    )
```

time: 97.3 us -> 109 us (1.12)
  waiting for transfers between devices: 59.3 us -> 75.8 us
  between operations: 0.89 us -> 14 us
  matrix products: 11.9 us -> 0 us
  Pallas kernels: 0 us -> 7.92 us
  other arithmetic: 7.4 us -> 0 us
  starting transfers between devices: 3.37 us -> 0.08 us
  local copies, waits for them, and re-layouts: 13.4 us -> 11.1 us
    all_gather x0 -> x2, waiting for transfers between devices: none -> 74.4 us  [the longest x1 44.4 us: on_device(): all_keys = lax.all_gather(keys, 'tm', axis=0, tiled=True)]
    ppermute x7 -> x0, waiting for transfers between devices: 59.3 us -> none  [from_behind(): return lax.ppermute(value, axis, pairs)]
    dot_general x16 -> x0, matrix products: 11.9 us -> none  [the longest x8 8.37 us: attend_block(): jnp.einsum('kgqn,nkd->kgqd', weight.astype(jnp.bfloat16), values_three, p...]
    gather x11 -> x0, local copies, waits for them, and re-layouts: 8.87 us -> none  [the longest x7 4.51 us: hop(): jnp.take(row_mask, key_spans, axis=1) > 0]
    unnamed x16, local copies, waits for them, and re-layouts: 2.59 us -> 11.1 us
    pallas_call x0 -> x2, Pallas kernels: none -> 7.92 us  [the longest x1 5.36 us: on_device(): pl.pallas_call(weigh, out_shape=(jax.ShapeDtypeStruct((kv_heads, total, g...]
    ppermute x7 -> x0, starting transfers between devices: 3.37 us -> none  [from_behind(): return lax.ppermute(value, axis, pairs)]
    and x8 -> x0, other arithmetic: 2.62 us -> none  [the longest x1 2.49 us: on_device(): gate_rows = jnp.take(section_gate, jnp.take(section, query_spans), axis=0)]
  transfers between devices with their start and end apart: 7 -> 2, of which waited for: 7 -> 2; matrix products, arithmetic and copies ran while one was open for 6% -> 0% of each run, Pallas kernels for 0% -> 5%
where the time goes in v3:
time: 109 us
  waiting for transfers between devices  75.8 us (70%)
  between operations  14 us (13%)
  local copies, waits for them, and re-layouts  11.1 us (10%)
  Pallas kernels  7.92 us (7%)
    all_gather x1, waiting for transfers between devices, on_device(): all_keys = lax.all_gather(keys, 'tm', axis=0, tiled=True)  44.4 us
    all_gather x1, waiting for transfers between devices, on_device(): all_values = lax.all_gather(values, 'tm', axis=0, tiled=True)  30 us
    unnamed x16, local copies, waits for them, and re-layouts  11.1 us
    pallas_call x1, Pallas kernels, on_device(): pl.pallas_call(weigh, out_shape=(jax.ShapeDtypeStruct((kv_heads, total, g...  5.36 us
    pallas_call x1, Pallas kernels, on_device(): pl.pallas_call(mix, out_shape=jax.ShapeDtypeStruct((rows, width), jnp.bfl...  2.56 us
  transfers between devices with their start and end apart: 2, of which 2 were waited for; matrix products, arithmetic and copies ran while one was open for 0% of the time, Pallas kernels for 5%

profile of v3, /device:TPU:0, one launch (start us, length us, event | category | flops | bytes accessed | tf_op | source)
XLA Modules:
  0.0 108.9 jit_solution(7354573039961920556)
XLA Ops:
  7.2 0.0 all-gather.3.cloned.1.call-start
  7.2 0.7 all-gather.3.cloned.1.call-update
  7.9 0.0 all-gather.5.cloned.1.call-start
  7.9 0.7 all-gather.5.cloned.1.call-update
  8.6 44.4 %all-gather.3.cloned.1.call-done.refs_2_ = bf16[1024,512]{1,0:T(8,128)(2,1)} async-done(((bf16[128,512]{1,0:T(8,128)(2,1)}), bf16[1024,512]{1,0:T(8,128)(2,1)}) %all-gather.3.cloned.1.call-update) | async-done | bytes 1048592 | tf_op jit(solution)/shard_map/all_gather | solution.py:73
  53.0 0.0 copy-start.5
  53.0 1.2 %copy-done.5 = bf16[1024,512]{1,0:T(8,128)(2,1)S(1)} copy-done((bf16[1024,512]{1,0:T(8,128)(2,1)S(1)}, bf16[1024,512]{1,0:T(8,128)(2,1)}, u32[]{:S(2)}) %copy-start.5) | copy-done | bytes 1048600
  54.2 0.0 copy-start.6
  54.2 1.1 %copy-done.6 = bf16[128,3072]{1,0:T(8,128)(2,1)S(1)} copy-done((bf16[128,3072]{1,0:T(8,128)(2,1)S(1)}, bf16[128,3072]{1,0:T(8,128)(2,1)}, u32[]{:S(2)}) %copy-start.6) | copy-done | bytes 786456
  55.4 0.0 copy-start.7
  55.4 0.7 copy-done.7
  56.0 5.4 %weigh.1 = (bf16[4,1024,768]{2,1,0:T(8,128)(2,1)S(1)}, f32[4,8,768]{2,1,0:T(8,128)S(1)}, f32[24,128]{1,0:T(8,128)}) custom-call(s32[4,4]{1,0:T(4,128)S(1)} %copy-done.7, bf16[128,3072]{1,0:T(8,128)(2,1)S(1)} %copy-done.6, bf16[1024,512]{1,0:T(8,128)(2,1)S(1)} %copy-done.5), custom_call_target="tpu_custom_call" | custom-call | flops 1610612736 | bytes 6291456 | tf_op jit(solution)/shard_map/weigh/pallas_call | solution.py:86
  61.4 0.0 copy-start
  61.4 2.6 %copy-done = bf16[4,1024,768]{2,1,0:T(8,128)(2,1)} copy-done((bf16[4,1024,768]{2,1,0:T(8,128)(2,1)}, bf16[4,1024,768]{2,1,0:T(8,128)(2,1)S(1)}, u32[]{:S(2)}) %copy-start) | copy-done | bytes 6291480
  64.0 30.0 %all-gather.5.cloned.1.call-done.refs_4_ = bf16[1024,512]{1,0:T(8,128)(2,1)} async-done(((bf16[128,512]{1,0:T(8,128)(2,1)}), bf16[1024,512]{1,0:T(8,128)(2,1)}) %all-gather.5.cloned.1.call-update) | async-done | bytes 1048592 | tf_op jit(solution)/shard_map/all_gather | solution.py:74
  94.1 0.0 copy-start.1
  94.1 2.8 %copy-done.1 = bf16[4,1024,768]{2,1,0:T(8,128)(2,1)S(1)} copy-done((bf16[4,1024,768]{2,1,0:T(8,128)(2,1)S(1)}, bf16[4,1024,768]{2,1,0:T(8,128)(2,1)}, u32[]{:S(2)}) %copy-start.1) | copy-done | bytes 6291480
  96.8 0.0 copy-start.2
  96.9 1.2 %copy-done.2 = bf16[1024,512]{1,0:T(8,128)(2,1)S(1)} copy-done((bf16[1024,512]{1,0:T(8,128)(2,1)S(1)}, bf16[1024,512]{1,0:T(8,128)(2,1)}, u32[]{:S(2)}) %copy-start.2) | copy-done | bytes 1048600
  98.1 0.0 copy-start.3
  98.1 0.8 copy-done.3
  98.9 0.0 copy-start.4
  98.9 0.7 copy-done.4
  99.5 2.6 %mix.1 = bf16[128,3072]{1,0:T(8,128)(2,1)} custom-call(s32[4]{0:T(128)S(1)} %copy-done.4, bf16[4,1024,768]{2,1,0:T(8,128)(2,1)S(1)} %copy-done.1, f32[4,8,768]{2,1,0:T(8,128)S(1)} %get-tuple-element.6.refs_2_, f32[4,3072]{1,0:T(4,128)S(1)} %copy-done.3, bf16[1024,512]{1,0:T(8,128)(2,1)S(1)} %copy-done.2), custom_call_target="tpu_custom_call" | custom-call | flops 1610612736 | bytes 6291456 | tf_op jit(solution)/shard_map/mix/pallas_call | solution.py:102
Async XLA Ops:
  7.2 45.8 %all-gather.3.cloned.1.call-start = ((), (), s32[]{:S(2)}) async-start(), calls=%async_computation | async-start | bytes 1179648 | tf_op jit(solution)/shard_map/all_gather | solution.py:73
  7.9 86.2 %all-gather.5.cloned.1.call-start = ((), (), s32[]{:S(2)}) async-start(), calls=%async_computation.1 | async-start | bytes 1179648 | tf_op jit(solution)/shard_map/all_gather | solution.py:74
  53.0 1.2 %copy-start.5 = (bf16[1024,512]{1,0:T(8,128)(2,1)S(1)}, bf16[1024,512]{1,0:T(8,128)(2,1)}, u32[]{:S(2)}) copy-start(bf16[1024,512]{1,0:T(8,128)(2,1)} %all-gather.3.cloned.1.call-done.refs_2_) | copy-start | bytes 3145732
  54.2 1.1 %copy-start.6 = (bf16[128,3072]{1,0:T(8,128)(2,1)S(1)}, bf16[128,3072]{1,0:T(8,128)(2,1)}, u32[]{:S(2)}) copy-start(bf16[128,3072]{1,0:T(8,128)(2,1)} %refs_1_.1) | copy-start | bytes 2359300
  55.4 0.7 copy-start.7
  61.4 2.6 %copy-start = (bf16[4,1024,768]{2,1,0:T(8,128)(2,1)}, bf16[4,1024,768]{2,1,0:T(8,128)(2,1)S(1)}, u32[]{:S(2)}) copy-start(bf16[4,1024,768]{2,1,0:T(8,128)(2,1)S(1)} %get-tuple-element.5.refs_1_) | copy-start | bytes 18874372
  94.1 2.8 %copy-start.1 = (bf16[4,1024,768]{2,1,0:T(8,128)(2,1)S(1)}, bf16[4,1024,768]{2,1,0:T(8,128)(2,1)}, u32[]{:S(2)}) copy-start(bf16[4,1024,768]{2,1,0:T(8,128)(2,1)} %copy-done) | copy-start | bytes 18874372
  96.8 1.2 %copy-start.2 = (bf16[1024,512]{1,0:T(8,128)(2,1)S(1)}, bf16[1024,512]{1,0:T(8,128)(2,1)}, u32[]{:S(2)}) copy-start(bf16[1024,512]{1,0:T(8,128)(2,1)} %all-gather.5.cloned.1.call-done.refs_4_) | copy-start | bytes 3145732
  98.1 0.8 copy-start.3
  98.9 0.7 copy-start.4
Sparse Core Ops, SparseCore 0:
  10.1 42.8 all-gather.2
  55.1 38.8 all-gather.4
